TPU v7x, 512 devices: a whole 4x4x16 slice. The times are simulated.
512 devices in a mesh: row: 32 (over x_lo, z), col: 16 (over y, x_hi, core).
Axes of the slice: x: 4 (x_hi: 2, x_lo: 2; x = x_hi * 2 + x_lo), y: 4, z: 16, core: 2. Of those that a mesh axis runs over, the one named last changes fastest.
Arguments:
- inputs: bfloat16 [512, 20480], P('row', 'col'), may hold values from -6 to 6
- weight: bfloat16 [20480, 20480], P('col', 'row'), may hold values from -0.0390625 to 0.0390625
- out_grad: bfloat16 [512, 20480], P('col', 'row'), may hold values from -6 to 6
Outputs:
- queries: bfloat16 [512, 20480], P('col', 'row')
- input_grad: bfloat16 [512, 20480], P('row', 'col')
- weight_grad: bfloat16 [20480, 20480], P('col', 'row')
All inputs are finite; a program needn't handle non-finite values.
Results may differ from a plain program's by a relative error of at most 0.001.
Values may be sent and summed in bfloat16 or wider, within the bound.
No kernel may reach another device: no remote copies, remote signals or barrier semaphores. Data moves between devices by JAX's collectives and lax.ppermute only.
A program may use at most 64 MiB of HBM per device.

v0:
```python
import jax
import jax.numpy as jnp
from jax import lax
from jax.sharding import PartitionSpec as P


def on_device(inputs, weight, out_grad):
    gathered = lax.all_gather(inputs, "row", axis=0, tiled=True)
    rows = gathered
    queries = lax.psum_scatter(
        jnp.dot(rows, weight, preferred_element_type=jnp.float32),
        "col",
        scatter_dimension=0,
        tiled=True,
    ).astype(jnp.bfloat16)
    grad_all = lax.all_gather(out_grad, "col", axis=0, tiled=True)
    rows = grad_all
    input_grad = lax.psum_scatter(
        lax.dot_general(rows, weight, (((1,), (1,)), ((), ())), preferred_element_type=jnp.float32),
        "row",
        scatter_dimension=0,
        tiled=True,
    ).astype(jnp.bfloat16)
    scale = 1.0 / jnp.sqrt(jnp.float32(grad_all.shape[0]))
    product = lax.dot_general(
        gathered, grad_all, (((0,), (0,)), ((), ())), preferred_element_type=jnp.float32
    )
    weight_grad = (product * scale).astype(jnp.bfloat16)
    return (queries, input_grad, weight_grad)


def solution(mesh):
    placed = (P("row", "col"), P("col", "row"), P("col", "row"))
    return jax.shard_map(
        on_device,
        mesh=mesh,
        in_specs=placed,
        out_specs=(P("col", "row"), P("row", "col"), P("col", "row")),
        check_vma=False,
    )
```

profile of v0, /device:TPU:6, one launch (start us, length us, event | category | flops | bytes accessed | tf_op | source)
XLA Modules:
  0.0 385.4 jit_solution(15095890823473143223)
XLA Ops:
  7.2 0.0 copy-start
  7.2 0.0 all-gather.2.cloned.1.call-start
  7.2 0.7 all-gather.2.cloned.1.call-update
  7.9 0.0 copy-start.1
  7.9 0.0 reduce-scatter.3.cloned.1.call-start
  8.0 138.5 %all-gather.2.cloned.1.call-done = bf16[512,1280]{1,0:T(8,128)(2,1)} async-done(((bf16[16,1280]{1,0:T(8,128)(2,1)}), bf16[512,1280]{1,0:T(8,128)(2,1)}) %all-gather.2.cloned.1.call-update) | async-done | bytes 1310736 | tf_op jit(solution)/shard_map/all_gather | solution.py:8
  146.5 0.0 copy-done
  146.5 3.6 fusion.1
  150.1 0.0 reduce-scatter.3.cloned.1.call-update
  150.1 0.0 reduce-scatter.5.cloned.1.call-start
  150.2 0.0 copy-done.1
  150.2 22.7 %all_gather.7 = bf16[512,640]{1,0:T(8,128)(2,1)S(1)} all-gather(bf16[32,640]{1,0:T(8,128)(2,1)S(1)} %copy-done.1), channel_id=1, replica_groups=mesh['row'=32,'col'=16] {'col'}, dimensions={0}, use_global_device_ids=true | all-gather | bytes 696320 | tf_op jit(solution)/shard_map/all_gather | solution.py:16
  172.9 2.7 fusion.2
  175.6 0.0 reduce-scatter.5.cloned.1.call-update
  175.7 3.7 fusion
  179.4 55.8 %reduce-scatter.3.cloned.1.call-done = f32[32,640]{1,0:T(8,128)} async-done(((f32[512,640]{1,0:T(8,128)}), f32[32,640]{1,0:T(8,128)}) %reduce-scatter.3.cloned.1.call-update) | async-done | bytes 81936 | tf_op jit(solution)/shard_map/reduce_scatter | solution.py:10
  235.2 1.5 convert_element_type.9
  236.7 140.7 %reduce-scatter.5.cloned.1.call-done = f32[16,1280]{1,0:T(8,128)} async-done(((f32[512,1280]{1,0:T(8,128)}), f32[16,1280]{1,0:T(8,128)}) %reduce-scatter.5.cloned.1.call-update) | async-done | bytes 81936 | tf_op jit(solution)/shard_map/reduce_scatter | solution.py:18
  377.3 1.5 convert_element_type.10
Async XLA Ops:
  7.2 139.4 %copy-start = (bf16[1280,640]{1,0:T(8,128)(2,1)S(1)}, bf16[1280,640]{1,0:T(8,128)(2,1)}, u32[]{:S(2)}) copy-start(bf16[1280,640]{1,0:T(8,128)(2,1)} %param.4) | copy-start | bytes 4915204
  7.2 139.3 %all-gather.2.cloned.1.call-start = ((), (), s32[]{:S(2)}) async-start(), calls=%async_computation.2 | async-start | bytes 1351680 | tf_op jit(solution)/shard_map/all_gather | solution.py:8
  7.9 142.2 %copy-start.1 = (bf16[32,640]{1,0:T(8,128)(2,1)S(1)}, bf16[32,640]{1,0:T(8,128)(2,1)}, u32[]{:S(2)}) copy-start(bf16[32,640]{1,0:T(8,128)(2,1)} %param.5) | copy-start | bytes 122884
  7.9 227.2 %reduce-scatter.3.cloned.1.call-start = ((), (), s32[]{:S(2)}) async-start(), calls=%async_computation.3 | async-start | bytes 1392640 | tf_op jit(solution)/shard_map/reduce_scatter | solution.py:10
  150.1 227.2 %reduce-scatter.5.cloned.1.call-start = ((), (), s32[]{:S(2)}) async-start(), calls=%async_computation.4 | async-start | bytes 2703360 | tf_op jit(solution)/shard_map/reduce_scatter | solution.py:18
Sparse Core Ops, SparseCore 0:
  10.1 136.3 all-gather.1
  151.3 83.8 reduce-scatter.2
  238.2 139.0 reduce-scatter.4
where the time goes:
time: 386 us; the launch traced here: 385 us
  waiting for transfers between devices  336 us (87%)
  blocking collectives  22.7 us (6%)
  between operations  13.8 us (4%)
  matrix products  10 us (3%)
    reduce_scatter x1, waiting for transfers between devices, on_device(): lax.psum_scatter(lax.dot_general(rows, weight, (((1,), (1,)), ((), ())),...  141 us
    all_gather x1, waiting for transfers between devices, on_device(): gathered = lax.all_gather(inputs, 'row', axis=0, tiled=True)  139 us
    reduce_scatter x1, waiting for transfers between devices, on_device(): lax.psum_scatter(jnp.dot(rows, weight, preferred_element_type=jnp.float32...  55.8 us
    all_gather x1, blocking collectives, on_device(): grad_all = lax.all_gather(out_grad, 'col', axis=0, tiled=True)  22.7 us
  transfers between devices with their start and end apart: 3, of which 3 were waited for; matrix products, arithmetic and copies ran while one was open for 2% of the time, Pallas kernels for 0%

commit v1 on v0

v1 whole, which is shorter than its diff:
```python
import jax
import jax.numpy as jnp
from jax import lax
from jax.sharding import Mesh, PartitionSpec as P

ROW = ("xl", "z")
COL = ("y", "xh", "core")
PLANE = ("xl",) + COL
F32 = jnp.float32


def swap_pair(x):
    return lax.ppermute(x, "xl", [(0, 1), (1, 0)])


def gather(x, axes, n):
    return lax.all_to_all(jnp.broadcast_to(x[None], (n,) + x.shape), axes, 0, 0, tiled=True)


def on_device(inputs, weight, out_grad):
    xl = lax.axis_index("xl")
    weight_other = swap_pair(weight)
    grads = gather(out_grad, PLANE, 32).reshape(2, 512, 640)
    grad_own = lax.dynamic_index_in_dim(grads, xl, 0, keepdims=False)
    grad_other = lax.dynamic_index_in_dim(grads, 1 - xl, 0, keepdims=False)
    half = lambda g: lax.dynamic_slice_in_dim(g, xl * 256, 256, 0)
    nt = (((1,), (1,)), ((), ()))
    partial = lax.dot_general(half(grad_own), weight, nt, preferred_element_type=F32)
    partial += lax.dot_general(half(grad_other), weight_other, nt, preferred_element_type=F32)
    parts = lax.all_to_all(partial.reshape(16, 16, 1280), "z", 0, 0, tiled=True)
    input_grad = parts.sum(0).astype(jnp.bfloat16)

    own = gather(inputs, "z", 16).reshape(256, 1280)
    other = swap_pair(own)
    rows = jnp.where(xl == 0, jnp.concatenate([own, other]), jnp.concatenate([other, own]))
    q = jnp.dot(rows, weight, preferred_element_type=F32)
    q = lax.all_to_all(q.reshape(16, 32, 640), COL, 0, 0, tiled=True)
    queries = q.sum(0).astype(jnp.bfloat16)

    scale = 1.0 / jnp.sqrt(F32(512))
    product = lax.dot_general(rows, grad_own, (((0,), (0,)), ((), ())), preferred_element_type=F32)
    weight_grad = (product * scale).astype(jnp.bfloat16)
    return (queries, input_grad, weight_grad)


def solution(mesh):
    fine = Mesh(mesh.devices.reshape(2, 16, 4, 2, 2), ROW + COL)
    placed = (P(ROW, COL), P(COL, ROW), P(COL, ROW))
    return jax.shard_map(
        on_device,
        mesh=fine,
        in_specs=placed,
        out_specs=(P(COL, ROW), P(ROW, COL), P(COL, ROW)),
        check_vma=False,
    )
```

time: 386 us -> 213 us (0.55)
  waiting for transfers between devices: 336 us -> 116 us
  blocking collectives: 22.7 us -> 51.4 us
  starting transfers between devices: 0.12 us -> 25.2 us
  between operations: 13.8 us -> 0.7 us
    reduce_scatter x2 -> x0, waiting for transfers between devices: 196 us -> none  [the longest x1 141 us: on_device(): lax.psum_scatter(lax.dot_general(rows, weight, (((1,), (1,)), ((), ())),...]
    all_gather x1 -> x0, waiting for transfers between devices: 139 us -> none  [on_device(): gathered = lax.all_gather(inputs, 'row', axis=0, tiled=True)]
    all_to_all x0 -> x3, waiting for transfers between devices: none -> 69 us  [the longest x1 58.1 us: on_device(): parts = lax.all_to_all(partial.reshape(16, 16, 1280), 'z', 0, 0, tiled=True)]
    all_to_all x0 -> x1, blocking collectives: none -> 51.4 us  [gather(): lax.all_to_all(jnp.broadcast_to(x[None], (n,) + x.shape), axes, 0, 0, til...]
    ppermute x0 -> x2, waiting for transfers between devices: none -> 46.5 us  [swap_pair(): return lax.ppermute(x, 'xl', [(0, 1), (1, 0)])]
    all_gather x1 -> x0, blocking collectives: 22.7 us -> none  [on_device(): grad_all = lax.all_gather(out_grad, 'col', axis=0, tiled=True)]
    all_to_all x0 -> x3, starting transfers between devices: none -> 19.4 us  [the longest x1 7.57 us: gather(): lax.all_to_all(jnp.broadcast_to(x[None], (n,) + x.shape), axes, 0, 0, til...]
    ppermute x0 -> x2, starting transfers between devices: none -> 5.85 us  [swap_pair(): return lax.ppermute(x, 'xl', [(0, 1), (1, 0)])]
  transfers between devices with their start and end apart: 3 -> 5, of which waited for: 3 -> 4; matrix products, arithmetic and copies ran while one was open for 2% -> 7% of each run, Pallas kernels for 0% -> 0%
where the time goes in v1:
time: 213 us; the launch traced here: 209 us
  waiting for transfers between devices  116 us (54%)
  blocking collectives  51.4 us (24%)
  starting transfers between devices  25.2 us (12%)
  matrix products  13.2 us (6%)
    all_to_all x1, waiting for transfers between devices, on_device(): parts = lax.all_to_all(partial.reshape(16, 16, 1280), 'z', 0, 0, tiled=True)  58.1 us
    all_to_all x1, blocking collectives, gather(): lax.all_to_all(jnp.broadcast_to(x[None], (n,) + x.shape), axes, 0, 0, til...  51.4 us
    ppermute x2, waiting for transfers between devices, swap_pair(): return lax.ppermute(x, 'xl', [(0, 1), (1, 0)])  46.5 us
    all_to_all x1, waiting for transfers between devices, on_device(): q = lax.all_to_all(q.reshape(16, 32, 640), COL, 0, 0, tiled=True)  10.9 us
    all_to_all x1, starting transfers between devices, gather(): lax.all_to_all(jnp.broadcast_to(x[None], (n,) + x.shape), axes, 0, 0, til...  7.57 us
    all_to_all x1, starting transfers between devices, on_device(): q = lax.all_to_all(q.reshape(16, 32, 640), COL, 0, 0, tiled=True)  7.24 us
    ppermute x2, starting transfers between devices, swap_pair(): return lax.ppermute(x, 'xl', [(0, 1), (1, 0)])  5.85 us
    all_to_all x1, starting transfers between devices, on_device(): parts = lax.all_to_all(partial.reshape(16, 16, 1280), 'z', 0, 0, tiled=True)  4.59 us
  transfers between devices with their start and end apart: 5, of which 4 were waited for; matrix products, arithmetic and copies ran while one was open for 7% of the time, Pallas kernels for 0%

profile of v1, /device:TPU:6, one launch (start us, length us, event | category | flops | bytes accessed | tf_op | source)
XLA Modules:
  0.0 209.4 jit_solution(8031565353070990210)
XLA Ops:
  0.6 0.0 copy-start.1
  0.6 0.8 broadcast_in_dim.4
  1.5 51.4 %all_to_all.20 = bf16[16,16,1280]{2,1,0:T(8,128)(2,1)S(1)} all-to-all(bf16[16,16,1280]{2,1,0:T(8,128)(2,1)S(1)} %broadcast_in_dim.4), channel_id=1, replica_groups=mesh['xl'=2,'z'=16,'y'=4,'xh'=2,'core'=2] {'z'}, dimensions={0} | all-to-all | bytes 1310720 | tf_op jit(solution)/shard_map/all_to_all | solution.py:17
  52.9 0.0 copy-done.1
  52.9 1.2 broadcast_in_dim.5
  54.0 7.6 %all-to-all-start.2 = ((bf16[32,32,640]{2,1,0:T(8,128)(2,1)}), bf16[32,32,640]{2,1,0:T(8,128)(2,1)S(1)}, u32[]{:S(2)}, u32[]{:S(2)}) async-start(bf16[32,32,640]{2,1,0:T(8,128)(2,1)} %broadcast_in_dim.5), calls=%async_computation.2 | async-start | bytes 2621440 | tf_op jit(solution)/shard_map/all_to_all | solution.py:17
  61.6 2.8 %collective-permute-start = (bf16[256,1280]{1,0:T(8,128)(2,1)S(1)}, bf16[256,1280]{1,0:T(8,128)(2,1)S(1)}, u32[]{:S(2)}, u32[]{:S(2)}) collective-permute-start(bf16[256,1280]{1,0:T(8,128)(2,1)S(1)} %bitcast.20), channel_id=1, source_target_pairs={{0,256},{256,0},{1,257},{257,1},{2,258},{258,2},{3,259},{259,3},{4... | collective-permute-start | bytes 1966088 | tf_op jit(solution)/shard_map/ppermute | solution.py:13
  64.4 3.1 %collective-permute-start.1 = (bf16[1280,640]{1,0:T(8,128)(2,1)}, bf16[1280,640]{1,0:T(8,128)(2,1)}, u32[]{:S(2)}, u32[]{:S(2)}) collective-permute-start(bf16[1280,640]{1,0:T(8,128)(2,1)} %param.4), channel_id=1, source_target_pairs={{0,256},{256,0},{1,257},{257,1},{2,258},{258,2},{3,259},{259,3},{4... | collective-permute-start | bytes 4915208 | tf_op jit(solution)/shard_map/ppermute | solution.py:13
  67.5 24.6 %collective-permute-done = bf16[256,1280]{1,0:T(8,128)(2,1)S(1)} collective-permute-done((bf16[256,1280]{1,0:T(8,128)(2,1)S(1)}, bf16[256,1280]{1,0:T(8,128)(2,1)S(1)}, u32[]{:S(2)}, u32[]{:S(2)}) %collective-permute-start) | collective-permute-done | bytes 655392 | tf_op jit(solution)/shard_map/ppermute | solution.py:13
  92.1 0.0 copy-start.2
  92.1 3.9 %fusion.8 = f32[512,640]{1,0:T(8,128)} fusion(bf16[1280,640]{1,0:T(8,128)(2,1)} %param.4, bf16[256,1280]{1,0:T(8,128)(2,1)S(1)} %collective-permute-done, bf16[256,1280]{1,0:T(8,128)(2,1)S(1)} %bitcast.21, pred[]{:T(512)S(6)} %eq.3), kind=kOutput, calls=%fused_computation.11 | convolution fusion | flops 844759040 | bytes 4259841 | tf_op jit(solution)/shard_map/dot_general | solution.py:36
  96.0 0.0 copy-done.2
  96.0 0.0 all-to-all-done.2
  96.0 7.2 %all-to-all-start.1 = ((f32[16,32,640]{2,1,0:T(8,128)}), f32[16,32,640]{2,1,0:T(8,128)S(1)}, u32[]{:S(2)}, u32[]{:S(2)}) async-start(f32[16,32,640]{2,1,0:T(8,128)} %bitcast.19), calls=%async_computation.1 | async-start | bytes 2621440 | tf_op jit(solution)/shard_map/all_to_all | solution.py:37
  103.3 2.1 %fusion.4 = f32[256,1280]{1,0:T(8,128)S(1)} fusion(bf16[1280,640]{1,0:T(8,128)(2,1)} %param.4, bf16[2,512,640]{2,1,0:T(8,128)(2,1)S(1)} %bitcast.16, s32[]{:T(128)S(6)} %select_n.28, s32[]{:T(128)S(6)} %select_n.30), kind=kOutput, calls=%fused_computation.7 | convolution fusion | flops 419430400 | bytes 3276808 | tf_op jit(solution)/shard_map/dot_general | solution.py:28
  105.4 21.9 %collective-permute-done.1 = bf16[1280,640]{1,0:T(8,128)(2,1)} collective-permute-done((bf16[1280,640]{1,0:T(8,128)(2,1)}, bf16[1280,640]{1,0:T(8,128)(2,1)}, u32[]{:S(2)}, u32[]{:S(2)}) %collective-permute-start.1) | collective-permute-done | bytes 1638432 | tf_op jit(solution)/shard_map/ppermute | solution.py:13
  127.3 0.0 copy-done
  127.3 3.2 %convolution_add_fusion = f32[256,1280]{1,0:T(8,128)} fusion(f32[256,1280]{1,0:T(8,128)S(1)} %fusion.4, bf16[1280,640]{1,0:T(8,128)(2,1)} %collective-permute-done.1, bf16[2,512,640]{2,1,0:T(8,128)(2,1)S(1)} %bitcast.17, s32[]{:T(128)S(6)} %select_n.32, s32[]{:T(128)S(6)} %select_n.30), kind=kOutput, calls=%fused_computation.2 | convolution fusion | flops 419758080 | bytes 4587528 | tf_op jit(solution)/shard_map/dot_general | solution.py:29
  130.6 10.9 %all-to-all-done.1 = f32[16,32,640]{2,1,0:T(8,128)S(1)} async-done(((f32[16,32,640]{2,1,0:T(8,128)}), f32[16,32,640]{2,1,0:T(8,128)S(1)}, u32[]{:S(2)}, u32[]{:S(2)}) %all-to-all-start.1) | async-done | bytes 1310752 | tf_op jit(solution)/shard_map/all_to_all | solution.py:37
  141.4 4.6 %all-to-all-start.3 = ((f32[16,16,1280]{2,1,0:T(8,128)}), f32[16,16,1280]{2,1,0:T(8,128)S(1)}, u32[]{:S(2)}, u32[]{:S(2)}) async-start(f32[16,16,1280]{2,1,0:T(8,128)} %bitcast.5), calls=%async_computation.3 | async-start | bytes 2621440 | tf_op jit(solution)/shard_map/all_to_all | solution.py:30
  146.0 3.9 %fusion = bf16[1280,640]{1,0:T(8,128)(2,1)} fusion(bf16[2,512,640]{2,1,0:T(8,128)(2,1)} %bitcast.18, s32[]{:T(128)S(6)} %select_n.27, bf16[256,1280]{1,0:T(8,128)(2,1)} %copy-done.2, bf16[256,1280]{1,0:T(8,128)(2,1)S(1)} %bitcast.22, pred[]{:T(512)S(6)} %eq.3), kind=kOutput, calls=%fused_computation.1 | convolution fusion | flops 846397440 | bytes 3604485 | tf_op jit(solution)/shard_map/dot_general | solution.py:41
  149.9 0.7 reduce_sum.18
  150.6 58.1 %all-to-all-done.3 = f32[16,16,1280]{2,1,0:T(8,128)S(1)} async-done(((f32[16,16,1280]{2,1,0:T(8,128)}), f32[16,16,1280]{2,1,0:T(8,128)S(1)}, u32[]{:S(2)}, u32[]{:S(2)}) %all-to-all-start.3) | async-done | bytes 1310752 | tf_op jit(solution)/shard_map/all_to_all | solution.py:30
  208.7 0.7 reduce_sum.19
  (1 shorter events, 0.0 us)
Async XLA Ops:
  0.6 52.3 %copy-start.1 = (bf16[32,640]{1,0:T(8,128)(2,1)S(1)}, bf16[32,640]{1,0:T(8,128)(2,1)}, u32[]{:S(2)}) copy-start(bf16[32,640]{1,0:T(8,128)(2,1)} %param.5) | copy-start | bytes 122884
  54.0 42.0 %all-to-all-start.2 = ((bf16[32,32,640]{2,1,0:T(8,128)(2,1)}), bf16[32,32,640]{2,1,0:T(8,128)(2,1)S(1)}, u32[]{:S(2)}, u32[]{:S(2)}) async-start(bf16[32,32,640]{2,1,0:T(8,128)(2,1)} %broadcast_in_dim.5), calls=%async_computation.2 | async-start | bytes 2621440 | tf_op jit(solution)/shard_map/all_to_all | solution.py:17
  61.6 30.5 %collective-permute-start = (bf16[256,1280]{1,0:T(8,128)(2,1)S(1)}, bf16[256,1280]{1,0:T(8,128)(2,1)S(1)}, u32[]{:S(2)}, u32[]{:S(2)}) collective-permute-start(bf16[256,1280]{1,0:T(8,128)(2,1)S(1)} %bitcast.20), channel_id=1, source_target_pairs={{0,256},{256,0},{1,257},{257,1},{2,258},{258,2},{3,259},{259,3},{4... | collective-permute-start | bytes 1966088 | tf_op jit(solution)/shard_map/ppermute | solution.py:13
  64.4 63.0 %collective-permute-start.1 = (bf16[1280,640]{1,0:T(8,128)(2,1)}, bf16[1280,640]{1,0:T(8,128)(2,1)}, u32[]{:S(2)}, u32[]{:S(2)}) collective-permute-start(bf16[1280,640]{1,0:T(8,128)(2,1)} %param.4), channel_id=1, source_target_pairs={{0,256},{256,0},{1,257},{257,1},{2,258},{258,2},{3,259},{259,3},{4... | collective-permute-start | bytes 4915208 | tf_op jit(solution)/shard_map/ppermute | solution.py:13
  92.1 3.9 %copy-start.2 = (bf16[256,1280]{1,0:T(8,128)(2,1)}, bf16[256,1280]{1,0:T(8,128)(2,1)S(1)}, u32[]{:S(2)}) copy-start(bf16[256,1280]{1,0:T(8,128)(2,1)S(1)} %collective-permute-done) | copy-start | bytes 1966084
  96.0 31.3 %copy-start = (bf16[32,32,640]{2,1,0:T(8,128)(2,1)}, bf16[32,32,640]{2,1,0:T(8,128)(2,1)S(1)}, u32[]{:S(2)}) copy-start(bf16[32,32,640]{2,1,0:T(8,128)(2,1)S(1)} %all-to-all-done.2) | copy-start | bytes 3932164
  96.0 45.4 %all-to-all-start.1 = ((f32[16,32,640]{2,1,0:T(8,128)}), f32[16,32,640]{2,1,0:T(8,128)S(1)}, u32[]{:S(2)}, u32[]{:S(2)}) async-start(f32[16,32,640]{2,1,0:T(8,128)} %bitcast.19), calls=%async_computation.1 | async-start | bytes 2621440 | tf_op jit(solution)/shard_map/all_to_all | solution.py:37
  141.4 67.3 %all-to-all-start.3 = ((f32[16,16,1280]{2,1,0:T(8,128)}), f32[16,16,1280]{2,1,0:T(8,128)S(1)}, u32[]{:S(2)}, u32[]{:S(2)}) async-start(f32[16,16,1280]{2,1,0:T(8,128)} %bitcast.5), calls=%async_computation.3 | async-start | bytes 2621440 | tf_op jit(solution)/shard_map/all_to_all | solution.py:30

commit v2 on v1

v2 whole, which is shorter than its diff:
```python
import jax
import jax.numpy as jnp
from jax import lax
from jax.sharding import Mesh, PartitionSpec as P

ROW = ("xl", "z")
COL = ("yh", "yl", "xh", "core")
F32 = jnp.float32
BF16 = jnp.bfloat16
F16 = jnp.float16
NT = (((1,), (1,)), ((), ()))


def swap(x, axis):
    return lax.ppermute(x, axis, [(0, 1), (1, 0)])


def pick(x, i, axis):
    return lax.dynamic_index_in_dim(x, i, axis, keepdims=False)


def ordered(mine, other, i, axis):
    return jnp.where(i == 0, jnp.stack([mine, other], axis), jnp.stack([other, mine], axis))


def encode(rows):
    top = jnp.max(jnp.abs(rows), axis=-1, keepdims=True)
    power = jnp.clip(jnp.ceil(jnp.log2(top)), -100.0, 100.0)
    v = rows * jnp.exp2(-power)
    coded = (v * jnp.abs(v) * 8192.0).astype(F16)
    tail = jnp.broadcast_to(power.astype(F16), rows.shape[:-1] + (128,))
    return jnp.concatenate([coded, tail], axis=-1)


def decode(coded):
    u = coded[..., :-128].astype(F32)
    power = coded[..., -128:-127].astype(F32)
    return jnp.sign(u) * jnp.sqrt(jnp.abs(u) * (1.0 / 8192.0)) * jnp.exp2(power)


def on_device(inputs, weight, out_grad):
    xl, z, yh, yl, xh, core = (lax.axis_index(a) for a in ROW + COL)
    weight_other = swap(weight, "xl")

    spread = jnp.broadcast_to(out_grad[None], (32, 32, 640))
    grads = lax.all_to_all(spread, ("xl",) + COL, 0, 0, tiled=True).reshape(2, 512, 640)

    own = lax.all_gather(inputs, "z", axis=0, tiled=True)
    own, grads = lax.optimization_barrier((own, grads))

    grad_own, grad_other = pick(grads, xl, 0), pick(grads, 1 - xl, 0)
    half = lambda g: lax.dynamic_slice_in_dim(g, xl * 256, 256, 0)
    partial = lax.dot_general(half(grad_own), weight, NT, preferred_element_type=F32)
    partial += lax.dot_general(half(grad_other), weight_other, NT, preferred_element_type=F32)
    parts = lax.all_to_all(encode(partial.reshape(16, 16, 1280)), "z", 0, 0, tiled=True)
    input_grad = decode(parts).sum(0).astype(BF16)

    q = jnp.stack([jnp.dot(own, w, preferred_element_type=F32) for w in (weight, weight_other)])
    q = q.reshape(2, 2, 2, 2, 32, 640)
    for name, i, axis in (("core", core, 3), ("xh", xh, 2), ("yl", yl, 1)):
        q = pick(q, i, axis) + swap(pick(q, 1 - i, axis), name)
    own, q = lax.optimization_barrier((own, q))
    same = xl == yh
    first = lax.ppermute(jnp.where(same, q[1], q[0]), ("xl", "yh"), [(0, 2), (1, 0), (2, 3), (3, 1)])
    second = lax.ppermute(q[1], ("xl", "yh"), [(1, 2), (2, 1)])
    queries = (first + jnp.where(same, q[0], second)).astype(BF16)

    rows = ordered(own, swap(own, "xl"), xl, 0).reshape(512, 1280)
    scale = 1.0 / jnp.sqrt(F32(512))
    product = lax.dot_general(rows, grad_own, (((0,), (0,)), ((), ())), preferred_element_type=F32)
    weight_grad = (product * scale).astype(BF16)
    return (queries, input_grad, weight_grad)


def solution(mesh):
    fine = Mesh(mesh.devices.reshape(2, 16, 2, 2, 2, 2), ROW + COL)
    placed = (P(ROW, COL), P(COL, ROW), P(COL, ROW))
    return jax.shard_map(
        on_device,
        mesh=fine,
        in_specs=placed,
        out_specs=(P(COL, ROW), P(ROW, COL), P(COL, ROW)),
        check_vma=False,
    )
```

time: 213 us -> 137 us (0.64); the launches traced: 209 us -> 136 us
  waiting for transfers between devices: 116 us -> 34.4 us
  starting transfers between devices: 25.2 us -> 44 us
  blocking collectives: 51.4 us -> 36.8 us
  other arithmetic: 1.37 us -> 5.22 us
    all_to_all x3 -> x2, waiting for transfers between devices: 69 us -> 0.01 us  [the longest x1 0.01 us: on_device(): lax.all_to_all(spread, ('xl',) + COL, 0, 0, tiled=True).reshape(2, 512, 640)]
    all_to_all x1 -> x0, blocking collectives: 51.4 us -> none  [gather(): lax.all_to_all(jnp.broadcast_to(x[None], (n,) + x.shape), axes, 0, 0, til...]
    all_gather x0 -> x1, blocking collectives: none -> 36.8 us  [on_device(): own = lax.all_gather(inputs, 'z', axis=0, tiled=True)]
    ppermute x2 -> x7, starting transfers between devices: 5.85 us -> 21 us  [the longest x5 13.9 us: swap(): return lax.ppermute(x, axis, [(0, 1), (1, 0)])]
    ppermute x2 -> x7, waiting for transfers between devices: 46.5 us -> 34.4 us  [the longest x5 23.5 us: swap(): return lax.ppermute(x, axis, [(0, 1), (1, 0)])]
    all_to_all x3 -> x2, starting transfers between devices: 19.4 us -> 23 us  [the longest x1 12.7 us: on_device(): lax.all_to_all(encode(partial.reshape(16, 16, 1280)), 'z', 0, 0, tiled=True)]
    dot_general x3 -> x4, matrix products: 9.28 us -> 7.86 us  [the longest x1 3.34 us: on_device(): lax.dot_general(half(grad_other), weight_other, NT, preferred_element_typ...]
  transfers between devices with their start and end apart: 5 -> 9, of which waited for: 4 -> 4; matrix products, arithmetic and copies ran while one was open for 7% -> 7% of each run, Pallas kernels for 0% -> 0%
where the time goes in v2:
time: 137 us; the launch traced here: 136 us
  starting transfers between devices  44 us (32%)
  blocking collectives  36.8 us (27%)
  waiting for transfers between devices  34.4 us (25%)
  matrix products  11.3 us (8%)
  other arithmetic  5.22 us (4%)
  local copies, waits for them, and re-layouts  3.5 us (3%)
    all_gather x1, blocking collectives, on_device(): own = lax.all_gather(inputs, 'z', axis=0, tiled=True)  36.8 us
    ppermute x5, waiting for transfers between devices, swap(): return lax.ppermute(x, axis, [(0, 1), (1, 0)])  23.5 us
    ppermute x5, starting transfers between devices, swap(): return lax.ppermute(x, axis, [(0, 1), (1, 0)])  13.9 us
    all_to_all x1, starting transfers between devices, on_device(): lax.all_to_all(encode(partial.reshape(16, 16, 1280)), 'z', 0, 0, tiled=True)  12.7 us
    ppermute x1, waiting for transfers between devices, on_device(): second = lax.ppermute(q[1], ('xl', 'yh'), [(1, 2), (2, 1)])  10.9 us
    all_to_all x1, starting transfers between devices, on_device(): lax.all_to_all(spread, ('xl',) + COL, 0, 0, tiled=True).reshape(2, 512, 640)  10.4 us
    ppermute x1, starting transfers between devices, on_device(): second = lax.ppermute(q[1], ('xl', 'yh'), [(1, 2), (2, 1)])  5.16 us
    dot_general x1, matrix products, on_device(): lax.dot_general(rows, grad_own, (((0,), (0,)), ((), ())), preferred_eleme...  3.49 us
  transfers between devices with their start and end apart: 9, of which 4 were waited for; matrix products, arithmetic and copies ran while one was open for 7% of the time, Pallas kernels for 0%

profile of v2, /device:TPU:6, one launch (start us, length us, event | category | flops | bytes accessed | tf_op | source)
XLA Modules:
  0.0 136.2 jit_solution(8939203186412122881)
XLA Ops:
  0.6 1.9 %broadcast_in_dim.4 = bf16[32,32,640]{2,1,0:T(8,128)(2,1)} broadcast(bf16[32,640]{1,0:T(8,128)(2,1)} %param.5), dimensions={1,2} | broadcast | bytes 1351680 | tf_op jit(solution)/shard_map/broadcast_in_dim | solution.py:45
  2.6 10.4 %all-to-all-start = ((bf16[32,32,640]{2,1,0:T(8,128)(2,1)}), bf16[32,32,640]{2,1,0:T(8,128)(2,1)}, u32[]{:S(2)}, u32[]{:S(2)}) async-start(bf16[32,32,640]{2,1,0:T(8,128)(2,1)} %broadcast_in_dim.4), calls=%async_computation | async-start | bytes 2621440 | tf_op jit(solution)/shard_map/all_to_all | solution.py:46
  13.0 2.7 %collective-permute-start = (bf16[1280,640]{1,0:T(8,128)(2,1)S(1)}, bf16[1280,640]{1,0:T(8,128)(2,1)}, u32[]{:S(2)}, u32[]{:S(2)}) collective-permute-start(bf16[1280,640]{1,0:T(8,128)(2,1)S(1)} %copy-done), channel_id=1, source_target_pairs={{0,256},{256,0},{1,257},{257,1},{2,258},{258,2},{3,259},{259,3},{4... | collective-permute-start | bytes 4915208 | tf_op jit(solution)/shard_map/ppermute | solution.py:15
  15.6 36.8 %all_gather.3 = bf16[256,1280]{1,0:T(8,128)(2,1)S(1)} all-gather(bf16[16,1280]{1,0:T(8,128)(2,1)S(1)} %copy-done.2), channel_id=1, replica_groups=mesh['xl'=2,'z'=16,'yh'=2,'yl'=2,'xh'=2,'core'=2] {'z'}, dimensions={0}, use_global_device_ids=true | all-gather | bytes 696320 | tf_op jit(solution)/shard_map/all_gather | solution.py:48
  53.1 1.7 %fusion.16 = f32[256,1280]{1,0:T(8,128)S(1)} fusion(bf16[1280,640]{1,0:T(8,128)(2,1)S(1)} %copy-done, bf16[2,512,640]{2,1,0:T(8,128)(2,1)} %bitcast, s32[]{:T(128)S(6)} %select_n.78, s32[]{:T(128)S(6)} %select_n.80), kind=kOutput, calls=%fused_computation.28 | convolution fusion | flops 419430400 | bytes 3276808 | tf_op jit(solution)/shard_map/dot_general | solution.py:53
  54.8 9.2 %collective-permute-done = bf16[1280,640]{1,0:T(8,128)(2,1)} collective-permute-done((bf16[1280,640]{1,0:T(8,128)(2,1)S(1)}, bf16[1280,640]{1,0:T(8,128)(2,1)}, u32[]{:S(2)}, u32[]{:S(2)}) %collective-permute-start) | collective-permute-done | bytes 1638432 | tf_op jit(solution)/shard_map/ppermute | solution.py:15
  64.0 3.3 %abs_reduce_fusion = (f32[256]{0:T(256)S(1)}, f32[256,1280]{1,0:T(8,128)}) fusion(f32[256,1280]{1,0:T(8,128)S(1)} %fusion.16, bf16[1280,640]{1,0:T(8,128)(2,1)} %collective-permute-done, bf16[2,512,640]{2,1,0:T(8,128)(2,1)} %bitcast, s32[]{:T(128)S(6)} %select_n.82, s32[]{:T(128)S(6)} %select_n.80), kind=kOutput, calls=%fused_computation.18 | convolution fusion | flops 420413184 | bytes 4588552 | tf_op jit(solution)/shard_map/dot_general | solution.py:54
  67.5 2.1 %fusion.27 = f32[256,640]{1,0:T(8,128)S(1)} fusion(bf16[256,1280]{1,0:T(8,128)(2,1)S(1)} %all_gather.3, bf16[1280,640]{1,0:T(8,128)(2,1)} %collective-permute-done), kind=kOutput, calls=%fused_computation.51 | convolution fusion | flops 419430400 | bytes 2949120 | tf_op jit(solution)/shard_map/dot_general | solution.py:58
  69.7 0.9 fusion.9
  70.6 1.9 %collective-permute-start.1 = (f32[2,2,2,32,640]{4,3,2,1,0:T(8,128)}, f32[2,2,2,32,640]{4,3,2,1,0:T(8,128)}, u32[]{:S(2)}, u32[]{:S(2)}) collective-permute-start(f32[2,2,2,32,640]{4,3,2,1,0:T(8,128)} %fusion.9), channel_id=1, source_target_pairs={{0,1},{1,0},{2,3},{3,2},{4,5},{5,4},{6,7},{7,6},{8,9},{9,8},{10,11... | collective-permute-start | bytes 1966088 | tf_op jit(solution)/shard_map/ppermute | solution.py:15
  72.9 1.0 pad_maximum_fusion
  74.0 12.7 %all-to-all-start.1 = ((f16[16,16,1408]{2,1,0:T(8,128)(2,1)}), f16[16,16,1408]{2,1,0:T(8,128)(2,1)S(1)}, u32[]{:S(2)}, u32[]{:S(2)}) async-start(f16[16,16,1408]{2,1,0:T(8,128)(2,1)} %pad_maximum_fusion), calls=%async_computation.1 | async-start | bytes 1441792 | tf_op jit(solution)/shard_map/all_to_all | solution.py:55
  86.7 1.2 fusion.12
  87.9 2.9 %collective-permute-start.2 = (f32[2,2,32,640]{3,2,0,1:T(8,128)S(1)}, f32[2,2,32,640]{3,2,0,1:T(8,128)S(1)}, u32[]{:S(2)}, u32[]{:S(2)}) collective-permute-start(f32[2,2,32,640]{3,2,0,1:T(8,128)S(1)} %bitcast.61), channel_id=1, source_target_pairs={{0,2},{2,0},{1,3},{3,1},{4,6},{6,4},{5,7},{7,5},{8,10},{10,8},{9,1... | collective-permute-start | bytes 983048 | tf_op jit(solution)/shard_map/ppermute | solution.py:15
  90.8 10.3 %collective-permute-done.2 = f32[2,2,32,640]{3,2,0,1:T(8,128)S(1)} collective-permute-done((f32[2,2,32,640]{3,2,0,1:T(8,128)S(1)}, f32[2,2,32,640]{3,2,0,1:T(8,128)S(1)}, u32[]{:S(2)}, u32[]{:S(2)}) %collective-permute-start.2) | collective-permute-done | bytes 327712 | tf_op jit(solution)/shard_map/ppermute | solution.py:15
  101.2 3.4 %collective-permute-start.3 = (f32[2,32,640]{2,1,0:T(8,128)S(1)}, f32[2,32,640]{2,1,0:T(8,128)S(1)}, u32[]{:S(2)}, u32[]{:S(2)}) collective-permute-start(f32[2,32,640]{2,1,0:T(8,128)S(1)} %dynamic-slice_bitcast_fusion), channel_id=1, source_target_pairs={{0,4},{4,0},{1,5},{5,1},{2,6},{6,2},{3,7},{7,3},{8,12},{12,8},{9,1... | collective-permute-start | bytes 491528 | tf_op jit(solution)/shard_map/ppermute | solution.py:15
  104.6 4.0 %collective-permute-done.3 = f32[2,32,640]{2,1,0:T(8,128)S(1)} collective-permute-done((f32[2,32,640]{2,1,0:T(8,128)S(1)}, f32[2,32,640]{2,1,0:T(8,128)S(1)}, u32[]{:S(2)}, u32[]{:S(2)}) %collective-permute-start.3) | collective-permute-done | bytes 163872 | tf_op jit(solution)/shard_map/ppermute | solution.py:15
  108.6 3.1 %collective-permute-start.6 = (bf16[256,1280]{1,0:T(8,128)(2,1)S(1)}, bf16[256,1280]{1,0:T(8,128)(2,1)S(1)}, u32[]{:S(2)}, u32[]{:S(2)}) collective-permute-start(bf16[256,1280]{1,0:T(8,128)(2,1)S(1)} %all_gather.3), channel_id=1, source_target_pairs={{0,256},{256,0},{1,257},{257,1},{2,258},{258,2},{3,259},{259,3},{4... | collective-permute-start | bytes 1966088 | tf_op jit(solution)/shard_map/ppermute | solution.py:15
  111.8 5.2 %collective-permute-start.5 = (f32[32,640]{1,0:T(8,128)S(1)}, f32[32,640]{1,0:T(8,128)S(1)}, u32[]{:S(2)}, u32[]{:S(2)}) collective-permute-start(f32[32,640]{1,0:T(8,128)S(1)} %slice_bitcast_fusion), channel_id=1, source_target_pairs={{8,256},{256,8},{9,257},{257,9},{10,258},{258,10},{11,259},{259,11... | collective-permute-start | bytes 245768 | tf_op jit(solution)/shard_map/ppermute | solution.py:65
  116.9 1.9 %collective-permute-start.4 = (f32[32,640]{1,0:T(8,128)S(1)}, f32[32,640]{1,0:T(8,128)S(1)}, u32[]{:S(2)}, u32[]{:S(2)}) collective-permute-start(f32[32,640]{1,0:T(8,128)S(1)} %bitcast_select_fusion.1), channel_id=1, source_target_pairs={{0,256},{8,0},{256,264},{264,8},{1,257},{9,1},{257,265},{265,9},{2... | collective-permute-start | bytes 245768 | tf_op jit(solution)/shard_map/ppermute | solution.py:64
  118.9 10.9 %collective-permute-done.5 = f32[32,640]{1,0:T(8,128)S(1)} collective-permute-done((f32[32,640]{1,0:T(8,128)S(1)}, f32[32,640]{1,0:T(8,128)S(1)}, u32[]{:S(2)}, u32[]{:S(2)}) %collective-permute-start.5) | collective-permute-done | bytes 81952 | tf_op jit(solution)/shard_map/ppermute | solution.py:65
  130.7 3.5 %fusion = bf16[1280,640]{1,0:T(8,128)(2,1)} fusion(bf16[512,1280]{1,0:T(8,128)(2,1)S(1)} %bitcast.59, bf16[2,512,640]{2,1,0:T(8,128)(2,1)} %bitcast, s32[]{:T(128)S(6)} %select_n.77), kind=kOutput, calls=%fused_computation.1 | convolution fusion | flops 840499200 | bytes 3604484 | tf_op jit(solution)/shard_map/dot_general | solution.py:70
  134.4 0.9 fusion.3
  135.4 0.8 copy.15
  (30 shorter events, 2.7 us)
Async XLA Ops:
  2.6 10.4 %copy-start = (bf16[1280,640]{1,0:T(8,128)(2,1)S(1)}, bf16[1280,640]{1,0:T(8,128)(2,1)}, u32[]{:S(2)}) copy-start(bf16[1280,640]{1,0:T(8,128)(2,1)} %param.4) | copy-start | bytes 4915204
  2.6 13.1 %copy-start.2 = (bf16[16,1280]{1,0:T(8,128)(2,1)S(1)}, bf16[16,1280]{1,0:T(8,128)(2,1)}, u32[]{:S(2)}) copy-start(bf16[16,1280]{1,0:T(8,128)(2,1)} %param.3) | copy-start | bytes 122884
  2.6 49.9 %all-to-all-start = ((bf16[32,32,640]{2,1,0:T(8,128)(2,1)}), bf16[32,32,640]{2,1,0:T(8,128)(2,1)}, u32[]{:S(2)}, u32[]{:S(2)}) async-start(bf16[32,32,640]{2,1,0:T(8,128)(2,1)} %broadcast_in_dim.4), calls=%async_computation | async-start | bytes 2621440 | tf_op jit(solution)/shard_map/all_to_all | solution.py:46
  13.0 51.0 %collective-permute-start = (bf16[1280,640]{1,0:T(8,128)(2,1)S(1)}, bf16[1280,640]{1,0:T(8,128)(2,1)}, u32[]{:S(2)}, u32[]{:S(2)}) collective-permute-start(bf16[1280,640]{1,0:T(8,128)(2,1)S(1)} %copy-done), channel_id=1, source_target_pairs={{0,256},{256,0},{1,257},{257,1},{2,258},{258,2},{3,259},{259,3},{4... | collective-permute-start | bytes 4915208 | tf_op jit(solution)/shard_map/ppermute | solution.py:15
  69.7 2.8 %copy-start.1 = (f32[256,1280]{1,0:T(8,128)S(1)}, f32[256,1280]{1,0:T(8,128)}, u32[]{:S(2)}) copy-start(f32[256,1280]{1,0:T(8,128)} %get-tuple-element.19) | copy-start | bytes 3932164
  70.6 16.1 %collective-permute-start.1 = (f32[2,2,2,32,640]{4,3,2,1,0:T(8,128)}, f32[2,2,2,32,640]{4,3,2,1,0:T(8,128)}, u32[]{:S(2)}, u32[]{:S(2)}) collective-permute-start(f32[2,2,2,32,640]{4,3,2,1,0:T(8,128)} %fusion.9), channel_id=1, source_target_pairs={{0,1},{1,0},{2,3},{3,2},{4,5},{5,4},{6,7},{7,6},{8,9},{9,8},{10,11... | collective-permute-start | bytes 1966088 | tf_op jit(solution)/shard_map/ppermute | solution.py:15
  74.0 60.2 %all-to-all-start.1 = ((f16[16,16,1408]{2,1,0:T(8,128)(2,1)}), f16[16,16,1408]{2,1,0:T(8,128)(2,1)S(1)}, u32[]{:S(2)}, u32[]{:S(2)}) async-start(f16[16,16,1408]{2,1,0:T(8,128)(2,1)} %pad_maximum_fusion), calls=%async_computation.1 | async-start | bytes 1441792 | tf_op jit(solution)/shard_map/all_to_all | solution.py:55
  87.9 13.2 %collective-permute-start.2 = (f32[2,2,32,640]{3,2,0,1:T(8,128)S(1)}, f32[2,2,32,640]{3,2,0,1:T(8,128)S(1)}, u32[]{:S(2)}, u32[]{:S(2)}) collective-permute-start(f32[2,2,32,640]{3,2,0,1:T(8,128)S(1)} %bitcast.61), channel_id=1, source_target_pairs={{0,2},{2,0},{1,3},{3,1},{4,6},{6,4},{5,7},{7,5},{8,10},{10,8},{9,1... | collective-permute-start | bytes 983048 | tf_op jit(solution)/shard_map/ppermute | solution.py:15
  101.2 7.4 %collective-permute-start.3 = (f32[2,32,640]{2,1,0:T(8,128)S(1)}, f32[2,32,640]{2,1,0:T(8,128)S(1)}, u32[]{:S(2)}, u32[]{:S(2)}) collective-permute-start(f32[2,32,640]{2,1,0:T(8,128)S(1)} %dynamic-slice_bitcast_fusion), channel_id=1, source_target_pairs={{0,4},{4,0},{1,5},{5,1},{2,6},{6,2},{3,7},{7,3},{8,12},{12,8},{9,1... | collective-permute-start | bytes 491528 | tf_op jit(solution)/shard_map/ppermute | solution.py:15
  108.6 21.8 %collective-permute-start.6 = (bf16[256,1280]{1,0:T(8,128)(2,1)S(1)}, bf16[256,1280]{1,0:T(8,128)(2,1)S(1)}, u32[]{:S(2)}, u32[]{:S(2)}) collective-permute-start(bf16[256,1280]{1,0:T(8,128)(2,1)S(1)} %all_gather.3), channel_id=1, source_target_pairs={{0,256},{256,0},{1,257},{257,1},{2,258},{258,2},{3,259},{259,3},{4... | collective-permute-start | bytes 1966088 | tf_op jit(solution)/shard_map/ppermute | solution.py:15
  111.8 18.0 %collective-permute-start.5 = (f32[32,640]{1,0:T(8,128)S(1)}, f32[32,640]{1,0:T(8,128)S(1)}, u32[]{:S(2)}, u32[]{:S(2)}) collective-permute-start(f32[32,640]{1,0:T(8,128)S(1)} %slice_bitcast_fusion), channel_id=1, source_target_pairs={{8,256},{256,8},{9,257},{257,9},{10,258},{258,10},{11,259},{259,11... | collective-permute-start | bytes 245768 | tf_op jit(solution)/shard_map/ppermute | solution.py:65
  116.9 12.9 %collective-permute-start.4 = (f32[32,640]{1,0:T(8,128)S(1)}, f32[32,640]{1,0:T(8,128)S(1)}, u32[]{:S(2)}, u32[]{:S(2)}) collective-permute-start(f32[32,640]{1,0:T(8,128)S(1)} %bitcast_select_fusion.1), channel_id=1, source_target_pairs={{0,256},{8,0},{256,264},{264,8},{1,257},{9,1},{257,265},{265,9},{2... | collective-permute-start | bytes 245768 | tf_op jit(solution)/shard_map/ppermute | solution.py:64

commit v3 on v2

v3 whole, which is shorter than its diff:
```python
import jax
import jax.numpy as jnp
from jax import lax
from jax.experimental import pallas as pl
from jax.experimental.pallas import tpu as pltpu
from jax.sharding import Mesh, PartitionSpec as P

ROW = ("xl", "z")
COL = ("yh", "yl", "xh", "core")
F32 = jnp.float32
BF16 = jnp.bfloat16
NT = (((1,), (1,)), ((), ()))


def swap(x, axis):
    return lax.ppermute(x, axis, [(0, 1), (1, 0)])


def pick(x, i, axis):
    return lax.dynamic_index_in_dim(x, i, axis, keepdims=False)


def ordered(mine, other, i, axis):
    return jnp.where(i == 0, jnp.stack([mine, other], axis), jnp.stack([other, mine], axis))


def encode_kernel(half, g_own, g_other, w_own, w_other, out):
    rows = lax.dot_general(g_own[0], w_own[...], NT, preferred_element_type=F32)
    rows += lax.dot_general(g_other[0], w_other[...], NT, preferred_element_type=F32)
    top = jnp.maximum(jnp.max(jnp.abs(rows), axis=-1, keepdims=True), 1e-30)
    power = jnp.clip(jnp.ceil(jnp.log2(top)), -100.0, 100.0)
    v = rows * jnp.exp2(-power)
    u = v * v
    u = u * u
    u = u * u * 2.0**60
    u = u * u
    out[:, :1280] = jnp.where(v < 0, -u, u).astype(BF16)
    out[:, 1280:] = jnp.broadcast_to(power, (rows.shape[0], 128)).astype(BF16)


def encode(grads, xl, weight, weight_other):
    tile = 128
    n = 256 // tile
    whole = pl.BlockSpec((1280, 640), lambda i, h: (0, 0))
    return pl.pallas_call(
        encode_kernel,
        grid_spec=pltpu.PrefetchScalarGridSpec(
            num_scalar_prefetch=1,
            grid=(n,),
            in_specs=[
                pl.BlockSpec((1, tile, 640), lambda i, h: (h[0], h[0] * n + i, 0)),
                pl.BlockSpec((1, tile, 640), lambda i, h: (1 - h[0], h[0] * n + i, 0)),
                whole,
                whole,
            ],
            out_specs=pl.BlockSpec((tile, 1408), lambda i, h: (i, 0)),
        ),
        out_shape=jax.ShapeDtypeStruct((256, 1408), BF16),
        compiler_params=pltpu.CompilerParams(vmem_limit_bytes=32 << 20),
        cost_estimate=pl.CostEstimate(flops=850_000_000, bytes_accessed=5_000_000, transcendentals=0),
    )(xl.reshape(1).astype(jnp.int32), grads, grads, weight, weight_other)


def decode_kernel(parts, out):
    total = jnp.zeros((16, 1280), F32)
    for i in range(16):
        u = parts[i, :, :1280].astype(F32)
        power = parts[i, :, 1280:].astype(F32)[:, :1]
        size = jnp.abs(u)
        root = jnp.exp2(jnp.log2(jnp.maximum(size, 1e-37)) * (1.0 / 16.0) + (power - 7.5))
        total += jnp.where(size > 1e-37, jnp.where(u < 0, -root, root), 0.0)
    out[...] = total.astype(BF16)


def decode(parts):
    return pl.pallas_call(
        decode_kernel,
        out_shape=jax.ShapeDtypeStruct((16, 1280), BF16),
        compiler_params=pltpu.CompilerParams(vmem_limit_bytes=32 << 20),
    )(parts)


def on_device(inputs, weight, out_grad):
    xl, z, yh, yl, xh, core = (lax.axis_index(a) for a in ROW + COL)
    weight_other = swap(weight, "xl")

    spread = jnp.broadcast_to(out_grad[None], (32, 32, 640))
    grads = lax.all_to_all(spread, ("xl",) + COL, 0, 0, tiled=True).reshape(2, 512, 640)

    own = lax.all_gather(inputs, "z", axis=0, tiled=True)
    own, weight_other = lax.optimization_barrier((own, weight_other))
    own_other = swap(own, "xl")
    by_core = own.reshape(2, 2, 2, 32, 1280)

    def project(i):
        x = pick(by_core, i, 2).reshape(128, 1280)
        return jnp.stack([jnp.dot(x, w, preferred_element_type=F32) for w in (weight, weight_other)])

    sent = project(1 - core)
    sent, grads = lax.optimization_barrier((sent, grads))
    parts = lax.all_to_all(encode(grads, xl, weight, weight_other).reshape(16, 16, 1408), "z", 0, 0, tiled=True)
    input_grad = decode(parts)

    q = (project(core) + swap(sent, "core")).reshape(2, 2, 2, 32, 640)
    own_other, q = lax.optimization_barrier((own_other, q))
    for name, i, axis in (("xh", xh, 2), ("yl", yl, 1)):
        q = pick(q, i, axis) + swap(pick(q, 1 - i, axis), name)
    same = xl == yh
    first = lax.ppermute(jnp.where(same, q[1], q[0]), ("xl", "yh"), [(0, 2), (1, 0), (2, 3), (3, 1)])
    second = lax.ppermute(q[1], ("xl", "yh"), [(1, 2), (2, 1)])
    queries = (first + jnp.where(same, q[0], second)).astype(BF16)

    rows = ordered(own, own_other, xl, 0).reshape(512, 1280)
    scale = 1.0 / jnp.sqrt(F32(512))
    grad_own = pick(grads, xl, 0)
    product = lax.dot_general(rows, grad_own, (((0,), (0,)), ((), ())), preferred_element_type=F32)
    weight_grad = (product * scale).astype(BF16)
    return (queries, input_grad, weight_grad)


def solution(mesh):
    fine = Mesh(mesh.devices.reshape(2, 16, 2, 2, 2, 2), ROW + COL)
    placed = (P(ROW, COL), P(COL, ROW), P(COL, ROW))
    return jax.shard_map(
        on_device,
        mesh=fine,
        in_specs=placed,
        out_specs=(P(COL, ROW), P(ROW, COL), P(COL, ROW)),
        check_vma=False,
    )
```

time: 137 us -> 122 us (0.89)
  waiting for transfers between devices: 34.4 us -> 14.5 us
  Pallas kernels: 0 us -> 6.32 us
  matrix products: 11.3 us -> 6.22 us
  starting transfers between devices: 44 us -> 46.4 us
    ppermute x5, waiting for transfers between devices: 23.5 us -> 10.8 us  [swap(): return lax.ppermute(x, axis, [(0, 1), (1, 0)])]
    ppermute x1, waiting for transfers between devices: 10.9 us -> 0.01 us  [on_device(): second = lax.ppermute(q[1], ('xl', 'yh'), [(1, 2), (2, 1)])]
    pallas_call x0 -> x2, Pallas kernels: none -> 6.32 us  [the longest x1 3.96 us: encode(): pl.pallas_call(encode_kernel, grid_spec=pltpu.PrefetchScalarGridSpec(num_...]
    dot_general x4, matrix products: 7.86 us -> 2.73 us  [project(): jnp.dot(x, w, preferred_element_type=F32)]
    all_to_all x1, waiting for transfers between devices: 0.01 us -> 2.57 us  [on_device(): lax.all_to_all(encode(grads, xl, weight, weight_other).reshape(16, 16, 14...]
    all_to_all x1, starting transfers between devices: 12.7 us -> 15.2 us  [on_device(): lax.all_to_all(encode(grads, xl, weight, weight_other).reshape(16, 16, 14...]
    ppermute x5, starting transfers between devices: 13.9 us -> 15.3 us  [swap(): return lax.ppermute(x, axis, [(0, 1), (1, 0)])]
  transfers between devices with their start and end apart: 9 -> 9, of which waited for: 4 -> 5; matrix products, arithmetic and copies ran while one was open for 7% -> 11% of each run, Pallas kernels for 0% -> 3%
where the time goes in v3:
time: 122 us; the launch traced here: 120 us
  starting transfers between devices  46.4 us (38%)
  blocking collectives  38 us (31%)
  waiting for transfers between devices  14.5 us (12%)
  Pallas kernels  6.32 us (5%)
  matrix products  6.22 us (5%)
  other arithmetic  4.29 us (4%)
  local copies, waits for them, and re-layouts  3.72 us (3%)
    all_gather x1, blocking collectives, on_device(): own = lax.all_gather(inputs, 'z', axis=0, tiled=True)  38 us
    ppermute x5, starting transfers between devices, swap(): return lax.ppermute(x, axis, [(0, 1), (1, 0)])  15.3 us
    all_to_all x1, starting transfers between devices, on_device(): lax.all_to_all(encode(grads, xl, weight, weight_other).reshape(16, 16, 14...  15.2 us
    ppermute x5, waiting for transfers between devices, swap(): return lax.ppermute(x, axis, [(0, 1), (1, 0)])  10.8 us
    all_to_all x1, starting transfers between devices, on_device(): lax.all_to_all(spread, ('xl',) + COL, 0, 0, tiled=True).reshape(2, 512, 640)  9.55 us
    ppermute x1, starting transfers between devices, on_device(): second = lax.ppermute(q[1], ('xl', 'yh'), [(1, 2), (2, 1)])  4.37 us
    pallas_call x1, Pallas kernels, encode(): pl.pallas_call(encode_kernel, grid_spec=pltpu.PrefetchScalarGridSpec(num_...  3.96 us
    dot_general x1, matrix products, on_device(): lax.dot_general(rows, grad_own, (((0,), (0,)), ((), ())), preferred_eleme...  3.49 us
  transfers between devices with their start and end apart: 9, of which 5 were waited for; matrix products, arithmetic and copies ran while one was open for 11% of the time, Pallas kernels for 3%

profile of v3, /device:TPU:6, one launch (start us, length us, event | category | flops | bytes accessed | tf_op | source)
XLA Modules:
  0.0 120.3 jit_solution(4569991085939886365)
XLA Ops:
  0.6 2.7 %collective-permute-start = (bf16[1280,640]{1,0:T(8,128)(2,1)}, bf16[1280,640]{1,0:T(8,128)(2,1)S(1)}, u32[]{:S(2)}, u32[]{:S(2)}) collective-permute-start(bf16[1280,640]{1,0:T(8,128)(2,1)} %w_own.1), channel_id=1, source_target_pairs={{0,256},{256,0},{1,257},{257,1},{2,258},{258,2},{3,259},{259,3},{4... | collective-permute-start | bytes 4915208 | tf_op jit(solution)/shard_map/ppermute | solution.py:16
  3.4 1.9 %broadcast_in_dim.2 = bf16[32,32,640]{2,1,0:T(8,128)(2,1)} broadcast(bf16[32,640]{1,0:T(8,128)(2,1)} %param.5), dimensions={1,2} | broadcast | bytes 1351680 | tf_op jit(solution)/shard_map/broadcast_in_dim | solution.py:87
  5.3 9.5 %all-to-all-start = ((bf16[32,32,640]{2,1,0:T(8,128)(2,1)}), bf16[32,32,640]{2,1,0:T(8,128)(2,1)}, u32[]{:S(2)}, u32[]{:S(2)}) async-start(bf16[32,32,640]{2,1,0:T(8,128)(2,1)} %broadcast_in_dim.2), calls=%async_computation | async-start | bytes 2621440 | tf_op jit(solution)/shard_map/all_to_all | solution.py:88
  14.9 38.0 %all_gather.3 = bf16[256,1280]{1,0:T(8,128)(2,1)S(1)} all-gather(bf16[16,1280]{1,0:T(8,128)(2,1)S(1)} %copy-done.5), channel_id=1, replica_groups=mesh['xl'=2,'z'=16,'yh'=2,'yl'=2,'xh'=2,'core'=2] {'z'}, dimensions={0}, use_global_device_ids=true | all-gather | bytes 696320 | tf_op jit(solution)/shard_map/all_gather | solution.py:90
  52.9 0.9 constant_dynamic-slice_fusion.1
  54.6 0.9 pad_maximum_fusion
  55.7 1.9 %collective-permute-start.2 = (f32[2,128,640]{2,1,0:T(8,128)}, f32[2,128,640]{2,1,0:T(8,128)}, u32[]{:S(2)}, u32[]{:S(2)}) collective-permute-start(f32[2,128,640]{2,1,0:T(8,128)} %pad_maximum_fusion), channel_id=1, source_target_pairs={{0,1},{1,0},{2,3},{3,2},{4,5},{5,4},{6,7},{7,6},{8,9},{9,8},{10,11... | collective-permute-start | bytes 1966088 | tf_op jit(solution)/shard_map/ppermute | solution.py:16
  57.7 2.8 %collective-permute-start.1 = (bf16[256,1280]{1,0:T(8,128)(2,1)}, bf16[256,1280]{1,0:T(8,128)(2,1)}, u32[]{:S(2)}, u32[]{:S(2)}) collective-permute-start(bf16[256,1280]{1,0:T(8,128)(2,1)} %copy-done.2), channel_id=1, source_target_pairs={{0,256},{256,0},{1,257},{257,1},{2,258},{258,2},{3,259},{259,3},{4... | collective-permute-start | bytes 1966088 | tf_op jit(solution)/shard_map/ppermute | solution.py:16
  60.5 4.0 %shard_map.58 = bf16[256,1408]{1,0:T(8,128)(2,1)S(1)} custom-call(s32[1]{0:T(128)} %bitcast.15.half, bf16[2,512,640]{2,1,0:T(8,128)(2,1)} %bitcast.7.g_own.g_other, bf16[2,512,640]{2,1,0:T(8,128)(2,1)} %bitcast.7.g_own.g_other, bf16[1280,640]{1,0:T(8,128)(2,1)S(1)} %copy-done, bf16[1280,640]{1,0:T(8,128)(2,1)S(1)} %collective-permute-done.w_other), custom_call_target="tpu_custom_call" | custom-call | flops 850000000 | bytes 5000000 | tf_op jit(solution)/shard_map/pallas_call | solution.py:45
  64.4 0.8 copy-done.1
  65.3 15.2 %all-to-all-start.1 = ((bf16[16,16,1408]{2,1,0:T(8,128)(2,1)}), bf16[16,16,1408]{2,1,0:T(8,128)(2,1)}, u32[]{:S(2)}, u32[]{:S(2)}) async-start(bf16[16,16,1408]{2,1,0:T(8,128)(2,1)} %bitcast.48), calls=%async_computation.1 | async-start | bytes 1441792 | tf_op jit(solution)/shard_map/all_to_all | solution.py:101
  80.5 1.5 %convolution_bitcast_fusion.2 = f32[1,128,640]{2,1,0:T(8,128)S(1)} fusion(bf16[128,1280]{1,0:T(8,128)(2,1)} %bitcast.51, bf16[1280,640]{1,0:T(8,128)(2,1)S(1)} %collective-permute-done.w_other), kind=kOutput, calls=%fused_computation.5 | convolution fusion | flops 209715200 | bytes 2293760 | tf_op jit(solution)/shard_map/dot_general | solution.py:97
  82.5 1.2 %maximum_add_fusion = f32[2,128,640]{2,1,0:T(8,128)S(1)} fusion(f32[2,128,640]{2,1,0:T(8,128)} %collective-permute-done.2, f32[1,128,640]{2,1,0:T(8,128)S(1)} %convolution_bitcast_fusion.2, f32[1,128,640]{2,1,0:T(8,128)S(1)} %convolution_bitcast_fusion.3), kind=kLoop, calls=%fused_computation.7 | loop fusion | flops 327680 | bytes 1966080 | tf_op jit(solution)/shard_map/add | solution.py:104
  83.7 4.5 %collective-permute-start.3 = (f32[2,2,32,640]{3,2,1,0:T(8,128)S(1)}, f32[2,2,32,640]{3,2,1,0:T(8,128)S(1)}, u32[]{:S(2)}, u32[]{:S(2)}) collective-permute-start(f32[2,2,32,640]{3,2,1,0:T(8,128)S(1)} %dynamic-slice_bitcast_fusion), channel_id=1, source_target_pairs={{0,2},{2,0},{1,3},{3,1},{4,6},{6,4},{5,7},{7,5},{8,10},{10,8},{9,1... | collective-permute-start | bytes 983048 | tf_op jit(solution)/shard_map/ppermute | solution.py:16
  88.2 8.5 %collective-permute-done.3 = f32[2,2,32,640]{3,2,1,0:T(8,128)S(1)} collective-permute-done((f32[2,2,32,640]{3,2,1,0:T(8,128)S(1)}, f32[2,2,32,640]{3,2,1,0:T(8,128)S(1)}, u32[]{:S(2)}, u32[]{:S(2)}) %collective-permute-start.3) | collective-permute-done | bytes 327712 | tf_op jit(solution)/shard_map/ppermute | solution.py:16
  96.8 3.4 %collective-permute-start.4 = (f32[2,32,640]{2,1,0:T(8,128)S(1)}, f32[2,32,640]{2,1,0:T(8,128)S(1)}, u32[]{:S(2)}, u32[]{:S(2)}) collective-permute-start(f32[2,32,640]{2,1,0:T(8,128)S(1)} %dynamic-slice_bitcast_fusion.1), channel_id=1, source_target_pairs={{0,4},{4,0},{1,5},{5,1},{2,6},{6,2},{3,7},{7,3},{8,12},{12,8},{9,1... | collective-permute-start | bytes 491528 | tf_op jit(solution)/shard_map/ppermute | solution.py:16
  100.2 1.5 %maximum_select_fusion = bf16[2,256,1280]{2,1,0:T(8,128)(2,1)S(1)} fusion(bf16[1,256,1280]{2,1,0:T(8,128)(2,1)} %bitcast.18, bf16[1,256,1280]{2,1,0:T(8,128)(2,1)S(1)} %bitcast.50, pred[]{:T(512)S(6)} %eq.7), kind=kLoop, calls=%fused_computation.2 | loop fusion | flops 1966080 | bytes 2621441 | tf_op jit(solution)/shard_map/jit(_where)/select_n | solution.py:24
  101.7 2.3 %collective-permute-done.4 = f32[2,32,640]{2,1,0:T(8,128)S(1)} collective-permute-done((f32[2,32,640]{2,1,0:T(8,128)S(1)}, f32[2,32,640]{2,1,0:T(8,128)S(1)}, u32[]{:S(2)}, u32[]{:S(2)}) %collective-permute-start.4) | collective-permute-done | bytes 163872 | tf_op jit(solution)/shard_map/ppermute | solution.py:16
  104.0 4.4 %collective-permute-start.6 = (f32[32,640]{1,0:T(8,128)S(1)}, f32[32,640]{1,0:T(8,128)S(1)}, u32[]{:S(2)}, u32[]{:S(2)}) collective-permute-start(f32[32,640]{1,0:T(8,128)S(1)} %slice_bitcast_fusion.1), channel_id=1, source_target_pairs={{8,256},{256,8},{9,257},{257,9},{10,258},{258,10},{11,259},{259,11... | collective-permute-start | bytes 245768 | tf_op jit(solution)/shard_map/ppermute | solution.py:110
  108.4 1.9 %collective-permute-start.5 = (f32[32,640]{1,0:T(8,128)S(1)}, f32[32,640]{1,0:T(8,128)S(1)}, u32[]{:S(2)}, u32[]{:S(2)}) collective-permute-start(f32[32,640]{1,0:T(8,128)S(1)} %fusion.3), channel_id=1, source_target_pairs={{0,256},{8,0},{256,264},{264,8},{1,257},{9,1},{257,265},{265,9},{2... | collective-permute-start | bytes 245768 | tf_op jit(solution)/shard_map/ppermute | solution.py:109
  110.3 3.5 %fusion = bf16[1280,640]{1,0:T(8,128)(2,1)} fusion(bf16[512,1280]{1,0:T(8,128)(2,1)S(1)} %bitcast.57, bf16[2,512,640]{2,1,0:T(8,128)(2,1)} %bitcast.7.g_own.g_other, s32[]{:T(128)S(6)} %select_n.67), kind=kOutput, calls=%fused_computation.1 | convolution fusion | flops 840499200 | bytes 3604484 | tf_op jit(solution)/shard_map/dot_general | solution.py:116
  113.8 0.9 collective-permute-done.5
  115.4 2.6 %all-to-all-done.1.parts = bf16[16,16,1408]{2,1,0:T(8,128)(2,1)} async-done(((bf16[16,16,1408]{2,1,0:T(8,128)(2,1)}), bf16[16,16,1408]{2,1,0:T(8,128)(2,1)}, u32[]{:S(2)}, u32[]{:S(2)}) %all-to-all-start.1) | async-done | bytes 720928 | tf_op jit(solution)/shard_map/all_to_all | solution.py:101
  118.0 2.4 %shard_map.59 = bf16[16,1280]{1,0:T(8,128)(2,1)} custom-call(bf16[16,16,1408]{2,1,0:T(8,128)(2,1)} %all-to-all-done.1.parts), custom_call_target="tpu_custom_call" | custom-call | tf_op jit(solution)/shard_map/pallas_call | solution.py:76
  (26 shorter events, 2.3 us)
Async XLA Ops:
  0.6 52.3 %collective-permute-start = (bf16[1280,640]{1,0:T(8,128)(2,1)}, bf16[1280,640]{1,0:T(8,128)(2,1)S(1)}, u32[]{:S(2)}, u32[]{:S(2)}) collective-permute-start(bf16[1280,640]{1,0:T(8,128)(2,1)} %w_own.1), channel_id=1, source_target_pairs={{0,256},{256,0},{1,257},{257,1},{2,258},{258,2},{3,259},{259,3},{4... | collective-permute-start | bytes 4915208 | tf_op jit(solution)/shard_map/ppermute | solution.py:16
  5.3 9.6 %copy-start.5 = (bf16[16,1280]{1,0:T(8,128)(2,1)S(1)}, bf16[16,1280]{1,0:T(8,128)(2,1)}, u32[]{:S(2)}) copy-start(bf16[16,1280]{1,0:T(8,128)(2,1)} %param.3) | copy-start | bytes 122884
  5.3 50.4 %all-to-all-start = ((bf16[32,32,640]{2,1,0:T(8,128)(2,1)}), bf16[32,32,640]{2,1,0:T(8,128)(2,1)}, u32[]{:S(2)}, u32[]{:S(2)}) async-start(bf16[32,32,640]{2,1,0:T(8,128)(2,1)} %broadcast_in_dim.2), calls=%async_computation | async-start | bytes 2621440 | tf_op jit(solution)/shard_map/all_to_all | solution.py:88
  14.9 38.9 %copy-start = (bf16[1280,640]{1,0:T(8,128)(2,1)S(1)}, bf16[1280,640]{1,0:T(8,128)(2,1)}, u32[]{:S(2)}) copy-start(bf16[1280,640]{1,0:T(8,128)(2,1)} %w_own.1) | copy-start | bytes 4915204
  52.9 1.3 %copy-start.2 = (bf16[256,1280]{1,0:T(8,128)(2,1)}, bf16[256,1280]{1,0:T(8,128)(2,1)S(1)}, u32[]{:S(2)}) copy-start(bf16[256,1280]{1,0:T(8,128)(2,1)S(1)} %all_gather.3) | copy-start | bytes 1966084
  55.7 26.7 %collective-permute-start.2 = (f32[2,128,640]{2,1,0:T(8,128)}, f32[2,128,640]{2,1,0:T(8,128)}, u32[]{:S(2)}, u32[]{:S(2)}) collective-permute-start(f32[2,128,640]{2,1,0:T(8,128)} %pad_maximum_fusion), channel_id=1, source_target_pairs={{0,1},{1,0},{2,3},{3,2},{4,5},{5,4},{6,7},{7,6},{8,9},{9,8},{10,11... | collective-permute-start | bytes 1966088 | tf_op jit(solution)/shard_map/ppermute | solution.py:16
  57.7 26.0 %collective-permute-start.1 = (bf16[256,1280]{1,0:T(8,128)(2,1)}, bf16[256,1280]{1,0:T(8,128)(2,1)}, u32[]{:S(2)}, u32[]{:S(2)}) collective-permute-start(bf16[256,1280]{1,0:T(8,128)(2,1)} %copy-done.2), channel_id=1, source_target_pairs={{0,256},{256,0},{1,257},{257,1},{2,258},{258,2},{3,259},{259,3},{4... | collective-permute-start | bytes 1966088 | tf_op jit(solution)/shard_map/ppermute | solution.py:16
  64.4 0.9 copy-start.1
  65.3 52.7 %all-to-all-start.1 = ((bf16[16,16,1408]{2,1,0:T(8,128)(2,1)}), bf16[16,16,1408]{2,1,0:T(8,128)(2,1)}, u32[]{:S(2)}, u32[]{:S(2)}) async-start(bf16[16,16,1408]{2,1,0:T(8,128)(2,1)} %bitcast.48), calls=%async_computation.1 | async-start | bytes 1441792 | tf_op jit(solution)/shard_map/all_to_all | solution.py:101
  80.5 1.5 %copy-start.4 = (bf16[2,2,1,32,1280]{4,3,2,1,0:T(8,128)(2,1)S(1)}, bf16[2,2,1,32,1280]{4,3,2,1,0:T(8,128)(2,1)}, u32[]{:S(2)}) copy-start(bf16[2,2,1,32,1280]{4,3,2,1,0:T(8,128)(2,1)} %get-tuple-element.15) | copy-start | bytes 983044
  82.4 17.7 %copy-start.3 = (bf16[256,1280]{1,0:T(8,128)(2,1)S(1)}, bf16[256,1280]{1,0:T(8,128)(2,1)}, u32[]{:S(2)}) copy-start(bf16[256,1280]{1,0:T(8,128)(2,1)} %copy-done.2) | copy-start | bytes 1966084
  83.7 13.0 %collective-permute-start.3 = (f32[2,2,32,640]{3,2,1,0:T(8,128)S(1)}, f32[2,2,32,640]{3,2,1,0:T(8,128)S(1)}, u32[]{:S(2)}, u32[]{:S(2)}) collective-permute-start(f32[2,2,32,640]{3,2,1,0:T(8,128)S(1)} %dynamic-slice_bitcast_fusion), channel_id=1, source_target_pairs={{0,2},{2,0},{1,3},{3,1},{4,6},{6,4},{5,7},{7,5},{8,10},{10,8},{9,1... | collective-permute-start | bytes 983048 | tf_op jit(solution)/shard_map/ppermute | solution.py:16
  96.8 7.2 %collective-permute-start.4 = (f32[2,32,640]{2,1,0:T(8,128)S(1)}, f32[2,32,640]{2,1,0:T(8,128)S(1)}, u32[]{:S(2)}, u32[]{:S(2)}) collective-permute-start(f32[2,32,640]{2,1,0:T(8,128)S(1)} %dynamic-slice_bitcast_fusion.1), channel_id=1, source_target_pairs={{0,4},{4,0},{1,5},{5,1},{2,6},{6,2},{3,7},{7,3},{8,12},{12,8},{9,1... | collective-permute-start | bytes 491528 | tf_op jit(solution)/shard_map/ppermute | solution.py:16
  104.0 9.8 %collective-permute-start.6 = (f32[32,640]{1,0:T(8,128)S(1)}, f32[32,640]{1,0:T(8,128)S(1)}, u32[]{:S(2)}, u32[]{:S(2)}) collective-permute-start(f32[32,640]{1,0:T(8,128)S(1)} %slice_bitcast_fusion.1), channel_id=1, source_target_pairs={{8,256},{256,8},{9,257},{257,9},{10,258},{258,10},{11,259},{259,11... | collective-permute-start | bytes 245768 | tf_op jit(solution)/shard_map/ppermute | solution.py:110
  108.4 6.3 %collective-permute-start.5 = (f32[32,640]{1,0:T(8,128)S(1)}, f32[32,640]{1,0:T(8,128)S(1)}, u32[]{:S(2)}, u32[]{:S(2)}) collective-permute-start(f32[32,640]{1,0:T(8,128)S(1)} %fusion.3), channel_id=1, source_target_pairs={{0,256},{8,0},{256,264},{264,8},{1,257},{9,1},{257,265},{265,9},{2... | collective-permute-start | bytes 245768 | tf_op jit(solution)/shard_map/ppermute | solution.py:109

commit v4 on v3

--- a/solution.py
+++ b/solution.py
@@ -24,7 +24,7 @@
     return jnp.where(i == 0, jnp.stack([mine, other], axis), jnp.stack([other, mine], axis))
 
 
-def encode_kernel(half, g_own, g_other, w_own, w_other, out):
+def encode_rows(g_own, g_other, w_own, w_other, out):
     rows = lax.dot_general(g_own[0], w_own[...], NT, preferred_element_type=F32)
     rows += lax.dot_general(g_other[0], w_other[...], NT, preferred_element_type=F32)
     top = jnp.maximum(jnp.max(jnp.abs(rows), axis=-1, keepdims=True), 1e-30)
@@ -34,31 +34,36 @@
     u = u * u
     u = u * u * 2.0**60
     u = u * u
-    out[:, :1280] = jnp.where(v < 0, -u, u).astype(BF16)
-    out[:, 1280:] = jnp.broadcast_to(power, (rows.shape[0], 128)).astype(BF16)
+    out[:, 0, :, :1280] = jnp.where(v < 0, -u, u).astype(BF16).reshape(4, 32, 1280)
+    out[:, 0, :, 1280:] = jnp.broadcast_to(power, (128, 128)).astype(BF16).reshape(4, 32, 128)
 
 
-def encode(grads, xl, weight, weight_other):
-    tile = 128
-    n = 256 // tile
-    whole = pl.BlockSpec((1280, 640), lambda i, h: (0, 0))
+def encode_kernel(place, g_own, g_other, s_own, s_other, w_own, w_other, out):
+    @pl.when(pl.program_id(0) == 0)
+    def _():
+        encode_rows(g_own, g_other, w_own, w_other, out)
+
+    @pl.when(pl.program_id(0) == 1)
+    def _():
+        encode_rows(s_own, s_other, w_own, w_other, out)
+
+
+def encode(mine, swapped, xl, core, weight, weight_other):
+    own = pl.BlockSpec((1, 128, 640), lambda i, at: (at[0], at[0], 0))
+    other = pl.BlockSpec((1, 128, 640), lambda i, at: (1 - at[0], at[0], 0))
+    whole = pl.BlockSpec((1280, 640), lambda i, at: (0, 0))
     return pl.pallas_call(
         encode_kernel,
         grid_spec=pltpu.PrefetchScalarGridSpec(
             num_scalar_prefetch=1,
-            grid=(n,),
-            in_specs=[
-                pl.BlockSpec((1, tile, 640), lambda i, h: (h[0], h[0] * n + i, 0)),
-                pl.BlockSpec((1, tile, 640), lambda i, h: (1 - h[0], h[0] * n + i, 0)),
-                whole,
-                whole,
-            ],
-            out_specs=pl.BlockSpec((tile, 1408), lambda i, h: (i, 0)),
+            grid=(2,),
+            in_specs=[own, other, own, other, whole, whole],
+            out_specs=pl.BlockSpec((4, 1, 32, 1408), lambda i, at: (0, at[1] + i - 2 * at[1] * i, 0, 0)),
         ),
-        out_shape=jax.ShapeDtypeStruct((256, 1408), BF16),
+        out_shape=jax.ShapeDtypeStruct((4, 2, 32, 1408), BF16),
         compiler_params=pltpu.CompilerParams(vmem_limit_bytes=32 << 20),
         cost_estimate=pl.CostEstimate(flops=850_000_000, bytes_accessed=5_000_000, transcendentals=0),
-    )(xl.reshape(1).astype(jnp.int32), grads, grads, weight, weight_other)
+    )(jnp.stack([xl, core]).astype(jnp.int32), mine, mine, swapped, swapped, weight, weight_other)
 
 
 def decode_kernel(parts, out):
@@ -84,24 +89,25 @@
     xl, z, yh, yl, xh, core = (lax.axis_index(a) for a in ROW + COL)
     weight_other = swap(weight, "xl")
 
-    spread = jnp.broadcast_to(out_grad[None], (32, 32, 640))
-    grads = lax.all_to_all(spread, ("xl",) + COL, 0, 0, tiled=True).reshape(2, 512, 640)
+    spread = jnp.broadcast_to(out_grad[None], (16, 32, 640))
+    grads = lax.all_to_all(spread, ("xl",) + COL[:3], 0, 0, tiled=True).reshape(2, 256, 640)
 
     own = lax.all_gather(inputs, "z", axis=0, tiled=True)
     own, weight_other = lax.optimization_barrier((own, weight_other))
-    own_other = swap(own, "xl")
-    by_core = own.reshape(2, 2, 2, 32, 1280)
-
-    def project(i):
-        x = pick(by_core, i, 2).reshape(128, 1280)
+    def project(rows, i):
+        x = pick(rows.reshape(2, 2, 2, 32, 1280), i, 2).reshape(128, 1280)
         return jnp.stack([jnp.dot(x, w, preferred_element_type=F32) for w in (weight, weight_other)])
 
-    sent = project(1 - core)
+    sent = project(own, 1 - core)
     sent, grads = lax.optimization_barrier((sent, grads))
-    parts = lax.all_to_all(encode(grads, xl, weight, weight_other).reshape(16, 16, 1408), "z", 0, 0, tiled=True)
+    swapped = swap(grads, "core")
+    coded = encode(grads, swapped, xl, core, weight, weight_other)
+    own_other = swap(own, "xl")
+    own, coded = lax.optimization_barrier((own, coded))
+    parts = lax.all_to_all(coded.reshape(16, 16, 1408), "z", 0, 0, tiled=True)
     input_grad = decode(parts)
 
-    q = (project(core) + swap(sent, "core")).reshape(2, 2, 2, 32, 640)
+    q = (project(own, core) + swap(sent, "core")).reshape(2, 2, 2, 32, 640)
     own_other, q = lax.optimization_barrier((own_other, q))
     for name, i, axis in (("xh", xh, 2), ("yl", yl, 1)):
         q = pick(q, i, axis) + swap(pick(q, 1 - i, axis), name)
@@ -112,7 +118,8 @@
 
     rows = ordered(own, own_other, xl, 0).reshape(512, 1280)
     scale = 1.0 / jnp.sqrt(F32(512))
-    grad_own = pick(grads, xl, 0)
+    grad_own = [pick(g, xl, 0).reshape(8, 32, 640) for g in (grads, swapped)]
+    grad_own = ordered(*grad_own, core, 1).reshape(512, 640)
     product = lax.dot_general(rows, grad_own, (((0,), (0,)), ((), ())), preferred_element_type=F32)
     weight_grad = (product * scale).astype(BF16)
     return (queries, input_grad, weight_grad)

time: 122 us -> 120 us (0.984)
  starting transfers between devices: 46.4 us -> 41.5 us
  matrix products: 6.22 us -> 4.11 us
  local copies, waits for them, and re-layouts: 3.72 us -> 5.66 us
  waiting for transfers between devices: 14.5 us -> 16 us
    all_to_all x2, starting transfers between devices: 24.8 us -> 20.4 us  [the longest x1 11.3 us: on_device(): parts = lax.all_to_all(coded.reshape(16, 16, 1408), 'z', 0, 0, tiled=True)]
    dynamic_slice x1 -> x4, local copies, waits for them, and re-layouts: 0.85 us -> 3.04 us  [pick(): return lax.dynamic_index_in_dim(x, i, axis, keepdims=False)]
    ppermute x5 -> x6, waiting for transfers between devices: 10.8 us -> 10.2 us  [swap(): return lax.ppermute(x, axis, [(0, 1), (1, 0)])]
    ppermute x5 -> x6, starting transfers between devices: 15.3 us -> 15.9 us  [swap(): return lax.ppermute(x, axis, [(0, 1), (1, 0)])]
  transfers between devices with their start and end apart: 9 -> 10, of which waited for: 5 -> 5; matrix products, arithmetic and copies ran while one was open for 11% -> 11% of each run, Pallas kernels for 3% -> 4%
where the time goes in v4:
time: 120 us; the launch traced here: 118 us
  starting transfers between devices  41.5 us (35%)
  blocking collectives  38.3 us (32%)
  waiting for transfers between devices  16 us (13%)
  Pallas kernels  7.13 us (6%)
  local copies, waits for them, and re-layouts  5.66 us (5%)
  other arithmetic  4.45 us (4%)
  matrix products  4.11 us (3%)
    all_gather x1, blocking collectives, on_device(): own = lax.all_gather(inputs, 'z', axis=0, tiled=True)  38.3 us
    ppermute x6, starting transfers between devices, swap(): return lax.ppermute(x, axis, [(0, 1), (1, 0)])  15.9 us
    all_to_all x1, starting transfers between devices, on_device(): parts = lax.all_to_all(coded.reshape(16, 16, 1408), 'z', 0, 0, tiled=True)  11.3 us
    ppermute x6, waiting for transfers between devices, swap(): return lax.ppermute(x, axis, [(0, 1), (1, 0)])  10.2 us
    all_to_all x1, starting transfers between devices, on_device(): lax.all_to_all(spread, ('xl',) + COL[:3], 0, 0, tiled=True)  9.08 us
    pallas_call x1, Pallas kernels, encode(): pl.pallas_call(encode_kernel, grid_spec=pltpu.PrefetchScalarGridSpec(num_...  4.77 us
    all_to_all x1, waiting for transfers between devices, on_device(): parts = lax.all_to_all(coded.reshape(16, 16, 1408), 'z', 0, 0, tiled=True)  3.78 us
    ppermute x1, starting transfers between devices, on_device(): second = lax.ppermute(q[1], ('xl', 'yh'), [(1, 2), (2, 1)])  3.34 us
  transfers between devices with their start and end apart: 10, of which 5 were waited for; matrix products, arithmetic and copies ran while one was open for 11% of the time, Pallas kernels for 4%

profile of v4, /device:TPU:6, one launch (start us, length us, event | category | flops | bytes accessed | tf_op | source)
XLA Modules:
  0.0 118.0 jit_solution(10878975369734428780)
XLA Ops:
  0.7 2.9 %collective-permute-start = (bf16[1280,640]{1,0:T(8,128)(2,1)}, bf16[1280,640]{1,0:T(8,128)(2,1)S(1)}, u32[]{:S(2)}, u32[]{:S(2)}) collective-permute-start(bf16[1280,640]{1,0:T(8,128)(2,1)} %w_own.1), channel_id=1, source_target_pairs={{0,256},{256,0},{1,257},{257,1},{2,258},{258,2},{3,259},{259,3},{4... | collective-permute-start | bytes 4915208 | tf_op jit(solution)/shard_map/ppermute | solution.py:16
  3.5 1.7 %broadcast_in_dim.2 = bf16[16,32,640]{2,1,0:T(8,128)(2,1)} broadcast(bf16[32,640]{1,0:T(8,128)(2,1)} %param.5), dimensions={1,2} | broadcast | bytes 696320 | tf_op jit(solution)/shard_map/broadcast_in_dim | solution.py:92
  5.2 9.1 %all-to-all-start = ((bf16[16,32,640]{2,1,0:T(8,128)(2,1)}), bf16[16,32,640]{2,1,0:T(8,128)(2,1)}, u32[]{:S(2)}, u32[]{:S(2)}) async-start(bf16[16,32,640]{2,1,0:T(8,128)(2,1)} %broadcast_in_dim.2), calls=%async_computation | async-start | bytes 1310720 | tf_op jit(solution)/shard_map/all_to_all | solution.py:93
  14.3 38.3 %all_gather.3 = bf16[256,1280]{1,0:T(8,128)(2,1)S(1)} all-gather(bf16[16,1280]{1,0:T(8,128)(2,1)S(1)} %copy-done.4), channel_id=1, replica_groups=mesh['xl'=2,'z'=16,'yh'=2,'yl'=2,'xh'=2,'core'=2] {'z'}, dimensions={0}, use_global_device_ids=true | all-gather | bytes 696320 | tf_op jit(solution)/shard_map/all_gather | solution.py:95
  54.4 1.9 %collective-permute-start.2 = (bf16[2,256,640]{2,1,0:T(8,128)(2,1)}, bf16[2,256,640]{2,1,0:T(8,128)(2,1)}, u32[]{:S(2)}, u32[]{:S(2)}) collective-permute-start(bf16[2,256,640]{2,1,0:T(8,128)(2,1)} %bitcast.6.g_own.g_other), channel_id=1, source_target_pairs={{0,1},{1,0},{2,3},{3,2},{4,5},{5,4},{6,7},{7,6},{8,9},{9,8},{10,11... | collective-permute-start | bytes 1966088 | tf_op jit(solution)/shard_map/ppermute | solution.py:16
  56.4 2.5 %collective-permute-start.1 = (bf16[256,1280]{1,0:T(8,128)(2,1)}, bf16[256,1280]{1,0:T(8,128)(2,1)}, u32[]{:S(2)}, u32[]{:S(2)}) collective-permute-start(bf16[256,1280]{1,0:T(8,128)(2,1)} %copy-done.2), channel_id=1, source_target_pairs={{0,256},{256,0},{1,257},{257,1},{2,258},{258,2},{3,259},{259,3},{4... | collective-permute-start | bytes 1966088 | tf_op jit(solution)/shard_map/ppermute | solution.py:16
  58.8 2.1 %collective-permute-start.3 = (f32[2,128,640]{2,1,0:T(8,128)}, f32[2,128,640]{2,1,0:T(8,128)}, u32[]{:S(2)}, u32[]{:S(2)}) collective-permute-start(f32[2,128,640]{2,1,0:T(8,128)} %pad_maximum_fusion), channel_id=1, source_target_pairs={{0,1},{1,0},{2,3},{3,2},{4,5},{5,4},{6,7},{7,6},{8,9},{9,8},{10,11... | collective-permute-start | bytes 1966088 | tf_op jit(solution)/shard_map/ppermute | solution.py:16
  61.0 4.8 %shard_map.58 = bf16[4,2,32,1408]{3,2,1,0:T(8,128)(2,1)S(1)} custom-call(s32[2]{0:T(128)S(1)} %pad_add_fusion.place, bf16[2,256,640]{2,1,0:T(8,128)(2,1)} %bitcast.6.g_own.g_other, bf16[2,256,640]{2,1,0:T(8,128)(2,1)} %bitcast.6.g_own.g_other, bf16[2,256,640]{2,1,0:T(8,128)(2,1)} %collective-permute-done.2.s_own.s_other, ...), custom_call_target="tpu_custom_call" | custom-call | flops 850000000 | bytes 5000000 | tf_op jit(solution)/shard_map/pallas_call | solution.py:55
  66.6 11.3 %all-to-all-start.1 = ((bf16[16,16,1408]{2,1,0:T(8,128)(2,1)}), bf16[16,16,1408]{2,1,0:T(8,128)(2,1)}, u32[]{:S(2)}, u32[]{:S(2)}) async-start(bf16[16,16,1408]{2,1,0:T(8,128)(2,1)} %bitcast.51), calls=%async_computation.1 | async-start | bytes 1441792 | tf_op jit(solution)/shard_map/all_to_all | solution.py:107
  77.9 1.0 constant_dynamic-slice_fusion.2
  79.8 1.2 %maximum_add_fusion = f32[2,128,640]{2,1,0:T(8,128)S(1)} fusion(f32[2,128,640]{2,1,0:T(8,128)} %collective-permute-done.3, f32[1,128,640]{2,1,0:T(8,128)S(1)} %convolution_bitcast_fusion, f32[1,128,640]{2,1,0:T(8,128)S(1)} %convolution_bitcast_fusion.1), kind=kLoop, calls=%fused_computation.8 | loop fusion | flops 327680 | bytes 1966080 | tf_op jit(solution)/shard_map/add | solution.py:110
  81.1 4.4 %collective-permute-start.4 = (f32[2,2,32,640]{3,2,1,0:T(8,128)S(1)}, f32[2,2,32,640]{3,2,1,0:T(8,128)S(1)}, u32[]{:S(2)}, u32[]{:S(2)}) collective-permute-start(f32[2,2,32,640]{3,2,1,0:T(8,128)S(1)} %dynamic-slice_bitcast_fusion), channel_id=1, source_target_pairs={{0,2},{2,0},{1,3},{3,1},{4,6},{6,4},{5,7},{7,5},{8,10},{10,8},{9,1... | collective-permute-start | bytes 983048 | tf_op jit(solution)/shard_map/ppermute | solution.py:16
  85.5 1.0 constant_dynamic-slice_fusion.1
  86.5 1.5 %maximum_select_fusion = bf16[2,256,1280]{2,1,0:T(8,128)(2,1)S(1)} fusion(bf16[1,256,1280]{2,1,0:T(8,128)(2,1)} %bitcast.20, bf16[1,256,1280]{2,1,0:T(8,128)(2,1)S(1)} %bitcast.54, pred[]{:T(512)S(6)} %eq.10), kind=kLoop, calls=%fused_computation.2 | loop fusion | flops 1966080 | bytes 2621441 | tf_op jit(solution)/shard_map/jit(_where)/select_n | solution.py:24
  88.0 6.1 %collective-permute-done.4 = f32[2,2,32,640]{3,2,1,0:T(8,128)S(1)} collective-permute-done((f32[2,2,32,640]{3,2,1,0:T(8,128)S(1)}, f32[2,2,32,640]{3,2,1,0:T(8,128)S(1)}, u32[]{:S(2)}, u32[]{:S(2)}) %collective-permute-start.4) | collective-permute-done | bytes 327712 | tf_op jit(solution)/shard_map/ppermute | solution.py:16
  94.2 2.1 %collective-permute-start.5 = (f32[2,32,640]{2,1,0:T(8,128)S(1)}, f32[2,32,640]{2,1,0:T(8,128)S(1)}, u32[]{:S(2)}, u32[]{:S(2)}) collective-permute-start(f32[2,32,640]{2,1,0:T(8,128)S(1)} %dynamic-slice_bitcast_fusion.1), channel_id=1, source_target_pairs={{0,4},{4,0},{1,5},{5,1},{2,6},{6,2},{3,7},{7,3},{8,12},{12,8},{9,1... | collective-permute-start | bytes 491528 | tf_op jit(solution)/shard_map/ppermute | solution.py:16
  96.4 1.0 constant_dynamic-slice_fusion
  97.5 4.0 %collective-permute-done.5 = f32[2,32,640]{2,1,0:T(8,128)S(1)} collective-permute-done((f32[2,32,640]{2,1,0:T(8,128)S(1)}, f32[2,32,640]{2,1,0:T(8,128)S(1)}, u32[]{:S(2)}, u32[]{:S(2)}) %collective-permute-start.5) | collective-permute-done | bytes 163872 | tf_op jit(solution)/shard_map/ppermute | solution.py:16
  101.5 3.3 %collective-permute-start.7 = (f32[32,640]{1,0:T(8,128)S(1)}, f32[32,640]{1,0:T(8,128)S(1)}, u32[]{:S(2)}, u32[]{:S(2)}) collective-permute-start(f32[32,640]{1,0:T(8,128)S(1)} %slice_bitcast_fusion.1), channel_id=1, source_target_pairs={{8,256},{256,8},{9,257},{257,9},{10,258},{258,10},{11,259},{259,11... | collective-permute-start | bytes 245768 | tf_op jit(solution)/shard_map/ppermute | solution.py:116
  104.9 1.9 %collective-permute-start.6 = (f32[32,640]{1,0:T(8,128)S(1)}, f32[32,640]{1,0:T(8,128)S(1)}, u32[]{:S(2)}, u32[]{:S(2)}) collective-permute-start(f32[32,640]{1,0:T(8,128)S(1)} %fusion.1), channel_id=1, source_target_pairs={{0,256},{8,0},{256,264},{264,8},{1,257},{9,1},{257,265},{265,9},{2... | collective-permute-start | bytes 245768 | tf_op jit(solution)/shard_map/ppermute | solution.py:115
  106.8 2.4 %fusion = bf16[1280,640]{1,0:T(8,128)(2,1)} fusion(bf16[512,1280]{1,0:T(8,128)(2,1)S(1)} %bitcast.61, bf16[512,640]{1,0:T(8,128)(2,1)S(1)} %bitcast.64), kind=kOutput, calls=%fused_computation.1 | convolution fusion | flops 840499200 | bytes 3604480 | tf_op jit(solution)/shard_map/dot_general | solution.py:123
  109.2 1.1 collective-permute-done.7
  111.8 3.8 %all-to-all-done.1.parts = bf16[16,16,1408]{2,1,0:T(8,128)(2,1)} async-done(((bf16[16,16,1408]{2,1,0:T(8,128)(2,1)}), bf16[16,16,1408]{2,1,0:T(8,128)(2,1)}, u32[]{:S(2)}, u32[]{:S(2)}) %all-to-all-start.1) | async-done | bytes 720928 | tf_op jit(solution)/shard_map/all_to_all | solution.py:107
  115.6 2.4 %shard_map.59 = bf16[16,1280]{1,0:T(8,128)(2,1)} custom-call(bf16[16,16,1408]{2,1,0:T(8,128)(2,1)} %all-to-all-done.1.parts), custom_call_target="tpu_custom_call" | custom-call | tf_op jit(solution)/shard_map/pallas_call | solution.py:81
  (31 shorter events, 5.4 us)
Async XLA Ops:
  0.6 52.0 %copy-start = (bf16[1280,640]{1,0:T(8,128)(2,1)S(1)}, bf16[1280,640]{1,0:T(8,128)(2,1)}, u32[]{:S(2)}) copy-start(bf16[1280,640]{1,0:T(8,128)(2,1)} %w_own.1) | copy-start | bytes 4915204
  0.6 13.7 %copy-start.4 = (bf16[16,1280]{1,0:T(8,128)(2,1)S(1)}, bf16[16,1280]{1,0:T(8,128)(2,1)}, u32[]{:S(2)}) copy-start(bf16[16,1280]{1,0:T(8,128)(2,1)} %param.3) | copy-start | bytes 122884
  0.7 51.9 %collective-permute-start = (bf16[1280,640]{1,0:T(8,128)(2,1)}, bf16[1280,640]{1,0:T(8,128)(2,1)S(1)}, u32[]{:S(2)}, u32[]{:S(2)}) collective-permute-start(bf16[1280,640]{1,0:T(8,128)(2,1)} %w_own.1), channel_id=1, source_target_pairs={{0,256},{256,0},{1,257},{257,1},{2,258},{258,2},{3,259},{259,3},{4... | collective-permute-start | bytes 4915208 | tf_op jit(solution)/shard_map/ppermute | solution.py:16
  5.2 49.2 %all-to-all-start = ((bf16[16,32,640]{2,1,0:T(8,128)(2,1)}), bf16[16,32,640]{2,1,0:T(8,128)(2,1)}, u32[]{:S(2)}, u32[]{:S(2)}) async-start(bf16[16,32,640]{2,1,0:T(8,128)(2,1)} %broadcast_in_dim.2), calls=%async_computation | async-start | bytes 1310720 | tf_op jit(solution)/shard_map/all_to_all | solution.py:93
  52.6 0.9 copy-start.2
  54.4 6.6 %collective-permute-start.2 = (bf16[2,256,640]{2,1,0:T(8,128)(2,1)}, bf16[2,256,640]{2,1,0:T(8,128)(2,1)}, u32[]{:S(2)}, u32[]{:S(2)}) collective-permute-start(bf16[2,256,640]{2,1,0:T(8,128)(2,1)} %bitcast.6.g_own.g_other), channel_id=1, source_target_pairs={{0,1},{1,0},{2,3},{3,2},{4,5},{5,4},{6,7},{7,6},{8,9},{9,8},{10,11... | collective-permute-start | bytes 1966088 | tf_op jit(solution)/shard_map/ppermute | solution.py:16
  56.4 24.7 %collective-permute-start.1 = (bf16[256,1280]{1,0:T(8,128)(2,1)}, bf16[256,1280]{1,0:T(8,128)(2,1)}, u32[]{:S(2)}, u32[]{:S(2)}) collective-permute-start(bf16[256,1280]{1,0:T(8,128)(2,1)} %copy-done.2), channel_id=1, source_target_pairs={{0,256},{256,0},{1,257},{257,1},{2,258},{258,2},{3,259},{259,3},{4... | collective-permute-start | bytes 1966088 | tf_op jit(solution)/shard_map/ppermute | solution.py:16
  58.8 21.0 %collective-permute-start.3 = (f32[2,128,640]{2,1,0:T(8,128)}, f32[2,128,640]{2,1,0:T(8,128)}, u32[]{:S(2)}, u32[]{:S(2)}) collective-permute-start(f32[2,128,640]{2,1,0:T(8,128)} %pad_maximum_fusion), channel_id=1, source_target_pairs={{0,1},{1,0},{2,3},{3,2},{4,5},{5,4},{6,7},{7,6},{8,9},{9,8},{10,11... | collective-permute-start | bytes 1966088 | tf_op jit(solution)/shard_map/ppermute | solution.py:16
  65.8 0.9 copy-start.1
  66.6 49.0 %all-to-all-start.1 = ((bf16[16,16,1408]{2,1,0:T(8,128)(2,1)}), bf16[16,16,1408]{2,1,0:T(8,128)(2,1)}, u32[]{:S(2)}, u32[]{:S(2)}) async-start(bf16[16,16,1408]{2,1,0:T(8,128)(2,1)} %bitcast.51), calls=%async_computation.1 | async-start | bytes 1441792 | tf_op jit(solution)/shard_map/all_to_all | solution.py:107
  79.8 6.7 %copy-start.3 = (bf16[256,1280]{1,0:T(8,128)(2,1)S(1)}, bf16[256,1280]{1,0:T(8,128)(2,1)}, u32[]{:S(2)}) copy-start(bf16[256,1280]{1,0:T(8,128)(2,1)} %copy-done.2) | copy-start | bytes 1966084
  81.1 13.0 %collective-permute-start.4 = (f32[2,2,32,640]{3,2,1,0:T(8,128)S(1)}, f32[2,2,32,640]{3,2,1,0:T(8,128)S(1)}, u32[]{:S(2)}, u32[]{:S(2)}) collective-permute-start(f32[2,2,32,640]{3,2,1,0:T(8,128)S(1)} %dynamic-slice_bitcast_fusion), channel_id=1, source_target_pairs={{0,2},{2,0},{1,3},{3,1},{4,6},{6,4},{5,7},{7,5},{8,10},{10,8},{9,1... | collective-permute-start | bytes 983048 | tf_op jit(solution)/shard_map/ppermute | solution.py:16
  94.2 7.3 %collective-permute-start.5 = (f32[2,32,640]{2,1,0:T(8,128)S(1)}, f32[2,32,640]{2,1,0:T(8,128)S(1)}, u32[]{:S(2)}, u32[]{:S(2)}) collective-permute-start(f32[2,32,640]{2,1,0:T(8,128)S(1)} %dynamic-slice_bitcast_fusion.1), channel_id=1, source_target_pairs={{0,4},{4,0},{1,5},{5,1},{2,6},{6,2},{3,7},{7,3},{8,12},{12,8},{9,1... | collective-permute-start | bytes 491528 | tf_op jit(solution)/shard_map/ppermute | solution.py:16
  101.5 8.7 %collective-permute-start.7 = (f32[32,640]{1,0:T(8,128)S(1)}, f32[32,640]{1,0:T(8,128)S(1)}, u32[]{:S(2)}, u32[]{:S(2)}) collective-permute-start(f32[32,640]{1,0:T(8,128)S(1)} %slice_bitcast_fusion.1), channel_id=1, source_target_pairs={{8,256},{256,8},{9,257},{257,9},{10,258},{258,10},{11,259},{259,11... | collective-permute-start | bytes 245768 | tf_op jit(solution)/shard_map/ppermute | solution.py:116
  104.9 6.3 %collective-permute-start.6 = (f32[32,640]{1,0:T(8,128)S(1)}, f32[32,640]{1,0:T(8,128)S(1)}, u32[]{:S(2)}, u32[]{:S(2)}) collective-permute-start(f32[32,640]{1,0:T(8,128)S(1)} %fusion.1), channel_id=1, source_target_pairs={{0,256},{8,0},{256,264},{264,8},{1,257},{9,1},{257,265},{265,9},{2... | collective-permute-start | bytes 245768 | tf_op jit(solution)/shard_map/ppermute | solution.py:115

commit v5 on v4

--- a/solution.py
+++ b/solution.py
@@ -24,9 +24,11 @@
     return jnp.where(i == 0, jnp.stack([mine, other], axis), jnp.stack([other, mine], axis))
 
 
-def encode_rows(g_own, g_other, w_own, w_other, out):
-    rows = lax.dot_general(g_own[0], w_own[...], NT, preferred_element_type=F32)
-    rows += lax.dot_general(g_other[0], w_other[...], NT, preferred_element_type=F32)
+def encode_kernel(place, g_own, g_other, s_own, s_other, w_own, w_other, out):
+    own = jnp.concatenate([g_own[0], s_own[0]], axis=0)
+    other = jnp.concatenate([g_other[0], s_other[0]], axis=0)
+    rows = lax.dot_general(own, w_own[...], NT, preferred_element_type=F32)
+    rows += lax.dot_general(other, w_other[...], NT, preferred_element_type=F32)
     top = jnp.maximum(jnp.max(jnp.abs(rows), axis=-1, keepdims=True), 1e-30)
     power = jnp.clip(jnp.ceil(jnp.log2(top)), -100.0, 100.0)
     v = rows * jnp.exp2(-power)
@@ -34,18 +36,12 @@
     u = u * u
     u = u * u * 2.0**60
     u = u * u
-    out[:, 0, :, :1280] = jnp.where(v < 0, -u, u).astype(BF16).reshape(4, 32, 1280)
-    out[:, 0, :, 1280:] = jnp.broadcast_to(power, (128, 128)).astype(BF16).reshape(4, 32, 128)
-
-
-def encode_kernel(place, g_own, g_other, s_own, s_other, w_own, w_other, out):
-    @pl.when(pl.program_id(0) == 0)
-    def _():
-        encode_rows(g_own, g_other, w_own, w_other, out)
-
-    @pl.when(pl.program_id(0) == 1)
-    def _():
-        encode_rows(s_own, s_other, w_own, w_other, out)
+    coded = jnp.where(v < 0, -u, u).astype(BF16)
+    tail = jnp.broadcast_to(power, (256, 128)).astype(BF16)
+    for i, core in enumerate((place[1], 1 - place[1])):
+        at = pl.ds(core, 1)
+        out[:, at, :, :1280] = coded[i * 128 : i * 128 + 128].reshape(4, 1, 32, 1280)
+        out[:, at, :, 1280:] = tail[i * 128 : i * 128 + 128].reshape(4, 1, 32, 128)
 
 
 def encode(mine, swapped, xl, core, weight, weight_other):
@@ -56,9 +52,9 @@
         encode_kernel,
         grid_spec=pltpu.PrefetchScalarGridSpec(
             num_scalar_prefetch=1,
-            grid=(2,),
+            grid=(1,),
             in_specs=[own, other, own, other, whole, whole],
-            out_specs=pl.BlockSpec((4, 1, 32, 1408), lambda i, at: (0, at[1] + i - 2 * at[1] * i, 0, 0)),
+            out_specs=pl.BlockSpec((4, 2, 32, 1408), lambda i, at: (0, 0, 0, 0)),
         ),
         out_shape=jax.ShapeDtypeStruct((4, 2, 32, 1408), BF16),
         compiler_params=pltpu.CompilerParams(vmem_limit_bytes=32 << 20),
@@ -66,11 +62,11 @@
     )(jnp.stack([xl, core]).astype(jnp.int32), mine, mine, swapped, swapped, weight, weight_other)
 
 
-def decode_kernel(parts, out):
-    total = jnp.zeros((16, 1280), F32)
+def decode_kernel(parts, powers, out):
+    total = jnp.zeros(out.shape, F32)
     for i in range(16):
-        u = parts[i, :, :1280].astype(F32)
-        power = parts[i, :, 1280:].astype(F32)[:, :1]
+        u = parts[i].astype(F32)
+        power = powers[i].astype(F32)[:, :1]
         size = jnp.abs(u)
         root = jnp.exp2(jnp.log2(jnp.maximum(size, 1e-37)) * (1.0 / 16.0) + (power - 7.5))
         total += jnp.where(size > 1e-37, jnp.where(u < 0, -root, root), 0.0)
@@ -80,9 +76,15 @@
 def decode(parts):
     return pl.pallas_call(
         decode_kernel,
+        grid=(2,),
+        in_specs=[
+            pl.BlockSpec((16, 16, 640), lambda i: (0, 0, i)),
+            pl.BlockSpec((16, 16, 128), lambda i: (0, 0, 10)),
+        ],
+        out_specs=pl.BlockSpec((16, 640), lambda i: (0, i)),
         out_shape=jax.ShapeDtypeStruct((16, 1280), BF16),
         compiler_params=pltpu.CompilerParams(vmem_limit_bytes=32 << 20),
-    )(parts)
+    )(parts, parts)
 
 
 def on_device(inputs, weight, out_grad):
@@ -103,14 +105,15 @@
     swapped = swap(grads, "core")
     coded = encode(grads, swapped, xl, core, weight, weight_other)
     own_other = swap(own, "xl")
-    own, coded = lax.optimization_barrier((own, coded))
+    own, grads, swapped, coded = lax.optimization_barrier((own, grads, swapped, coded))
     parts = lax.all_to_all(coded.reshape(16, 16, 1408), "z", 0, 0, tiled=True)
     input_grad = decode(parts)
 
     q = (project(own, core) + swap(sent, "core")).reshape(2, 2, 2, 32, 640)
     own_other, q = lax.optimization_barrier((own_other, q))
-    for name, i, axis in (("xh", xh, 2), ("yl", yl, 1)):
-        q = pick(q, i, axis) + swap(pick(q, 1 - i, axis), name)
+    piece = lambda j, k: pick(pick(q, k, 2), j, 1)
+    across = lax.ppermute(piece(1 - yl, 1 - xh), ("yl", "xh"), [(0, 3), (1, 2), (2, 1), (3, 0)])
+    q = piece(yl, xh) + swap(piece(yl, 1 - xh), "xh") + swap(piece(1 - yl, xh), "yl") + across
     same = xl == yh
     first = lax.ppermute(jnp.where(same, q[1], q[0]), ("xl", "yh"), [(0, 2), (1, 0), (2, 3), (3, 1)])
     second = lax.ppermute(q[1], ("xl", "yh"), [(1, 2), (2, 1)])

time: 120 us -> 118 us (0.983)
  starting transfers between devices: 41.5 us -> 46.9 us
  waiting for transfers between devices: 16 us -> 11.4 us
  Pallas kernels: 7.13 us -> 5.7 us
    ppermute x6, waiting for transfers between devices: 10.2 us -> 0.02 us  [swap(): return lax.ppermute(x, axis, [(0, 1), (1, 0)])]
    ppermute x0 -> x1, starting transfers between devices: none -> 3.99 us  [on_device(): lax.ppermute(piece(1 - yl, 1 - xh), ('yl', 'xh'), [(0, 3), (1, 2), (2, 1)...]
    ppermute x0 -> x1, waiting for transfers between devices: none -> 3.05 us  [on_device(): lax.ppermute(piece(1 - yl, 1 - xh), ('yl', 'xh'), [(0, 3), (1, 2), (2, 1)...]
    ppermute x1, waiting for transfers between devices: 1.06 us -> 3.86 us  [on_device(): second = lax.ppermute(q[1], ('xl', 'yh'), [(1, 2), (2, 1)])]
    ppermute x1, starting transfers between devices: 1.92 us -> 3.98 us  [on_device(): lax.ppermute(jnp.where(same, q[1], q[0]), ('xl', 'yh'), [(0, 2), (1, 0),...]
    pallas_call x1, Pallas kernels: 4.77 us -> 3.43 us  [encode(): pl.pallas_call(encode_kernel, grid_spec=pltpu.PrefetchScalarGridSpec(num_...]
    dynamic_slice x4 -> x3, local copies, waits for them, and re-layouts: 3.04 us -> 2.16 us  [pick(): return lax.dynamic_index_in_dim(x, i, axis, keepdims=False)]
  transfers between devices with their start and end apart: 10 -> 11, of which waited for: 5 -> 3; matrix products, arithmetic and copies ran while one was open for 11% -> 11% of each run, Pallas kernels for 4% -> 3%
where the time goes in v5:
time: 118 us; the launch traced here: 117 us
  starting transfers between devices  46.9 us (40%)
  blocking collectives  38.3 us (32%)
  waiting for transfers between devices  11.4 us (10%)
  Pallas kernels  5.7 us (5%)
  local copies, waits for them, and re-layouts  4.78 us (4%)
  other arithmetic  4.47 us (4%)
  matrix products  4.11 us (3%)
    all_gather x1, blocking collectives, on_device(): own = lax.all_gather(inputs, 'z', axis=0, tiled=True)  38.3 us
    ppermute x6, starting transfers between devices, swap(): return lax.ppermute(x, axis, [(0, 1), (1, 0)])  16.1 us
    all_to_all x1, starting transfers between devices, on_device(): parts = lax.all_to_all(coded.reshape(16, 16, 1408), 'z', 0, 0, tiled=True)  11.3 us
    all_to_all x1, starting transfers between devices, on_device(): lax.all_to_all(spread, ('xl',) + COL[:3], 0, 0, tiled=True)  9.09 us
    all_to_all x1, waiting for transfers between devices, on_device(): parts = lax.all_to_all(coded.reshape(16, 16, 1408), 'z', 0, 0, tiled=True)  4.47 us
    ppermute x1, starting transfers between devices, on_device(): lax.ppermute(piece(1 - yl, 1 - xh), ('yl', 'xh'), [(0, 3), (1, 2), (2, 1)...  3.99 us
    ppermute x1, starting transfers between devices, on_device(): lax.ppermute(jnp.where(same, q[1], q[0]), ('xl', 'yh'), [(0, 2), (1, 0),...  3.98 us
    ppermute x1, waiting for transfers between devices, on_device(): second = lax.ppermute(q[1], ('xl', 'yh'), [(1, 2), (2, 1)])  3.86 us
  transfers between devices with their start and end apart: 11, of which 3 were waited for; matrix products, arithmetic and copies ran while one was open for 11% of the time, Pallas kernels for 3%

profile of v5, /device:TPU:6, one launch (start us, length us, event | category | flops | bytes accessed | tf_op | source)
XLA Modules:
  0.0 116.6 jit_solution(4713577031630149432)
XLA Ops:
  0.7 2.9 %collective-permute-start = (bf16[1280,640]{1,0:T(8,128)(2,1)}, bf16[1280,640]{1,0:T(8,128)(2,1)S(1)}, u32[]{:S(2)}, u32[]{:S(2)}) collective-permute-start(bf16[1280,640]{1,0:T(8,128)(2,1)} %w_own.1), channel_id=1, source_target_pairs={{0,256},{256,0},{1,257},{257,1},{2,258},{258,2},{3,259},{259,3},{4... | collective-permute-start | bytes 4915208 | tf_op jit(solution)/shard_map/ppermute | solution.py:16
  3.5 1.7 %broadcast_in_dim.2 = bf16[16,32,640]{2,1,0:T(8,128)(2,1)} broadcast(bf16[32,640]{1,0:T(8,128)(2,1)} %param.5), dimensions={1,2} | broadcast | bytes 696320 | tf_op jit(solution)/shard_map/broadcast_in_dim | solution.py:94
  5.2 9.1 %all-to-all-start = ((bf16[16,32,640]{2,1,0:T(8,128)(2,1)}), bf16[16,32,640]{2,1,0:T(8,128)(2,1)}, u32[]{:S(2)}, u32[]{:S(2)}) async-start(bf16[16,32,640]{2,1,0:T(8,128)(2,1)} %broadcast_in_dim.2), calls=%async_computation | async-start | bytes 1310720 | tf_op jit(solution)/shard_map/all_to_all | solution.py:95
  14.3 38.3 %all_gather.3 = bf16[256,1280]{1,0:T(8,128)(2,1)S(1)} all-gather(bf16[16,1280]{1,0:T(8,128)(2,1)S(1)} %copy-done.4), channel_id=1, replica_groups=mesh['xl'=2,'z'=16,'yh'=2,'yl'=2,'xh'=2,'core'=2] {'z'}, dimensions={0}, use_global_device_ids=true | all-gather | bytes 696320 | tf_op jit(solution)/shard_map/all_gather | solution.py:97
  53.5 0.9 pad_maximum_fusion
  54.4 1.9 %collective-permute-start.2 = (bf16[2,256,640]{2,1,0:T(8,128)(2,1)}, bf16[2,256,640]{2,1,0:T(8,128)(2,1)}, u32[]{:S(2)}, u32[]{:S(2)}) collective-permute-start(bf16[2,256,640]{2,1,0:T(8,128)(2,1)} %bitcast.4.g_own.g_other), channel_id=1, source_target_pairs={{0,1},{1,0},{2,3},{3,2},{4,5},{5,4},{6,7},{7,6},{8,9},{9,8},{10,11... | collective-permute-start | bytes 1966088 | tf_op jit(solution)/shard_map/ppermute | solution.py:16
  56.4 2.5 %collective-permute-start.1 = (bf16[256,1280]{1,0:T(8,128)(2,1)}, bf16[256,1280]{1,0:T(8,128)(2,1)}, u32[]{:S(2)}, u32[]{:S(2)}) collective-permute-start(bf16[256,1280]{1,0:T(8,128)(2,1)} %copy-done.2), channel_id=1, source_target_pairs={{0,256},{256,0},{1,257},{257,1},{2,258},{258,2},{3,259},{259,3},{4... | collective-permute-start | bytes 1966088 | tf_op jit(solution)/shard_map/ppermute | solution.py:16
  58.9 2.1 %collective-permute-start.3 = (f32[2,128,640]{2,1,0:T(8,128)}, f32[2,128,640]{2,1,0:T(8,128)}, u32[]{:S(2)}, u32[]{:S(2)}) collective-permute-start(f32[2,128,640]{2,1,0:T(8,128)} %pad_maximum_fusion), channel_id=1, source_target_pairs={{0,1},{1,0},{2,3},{3,2},{4,5},{5,4},{6,7},{7,6},{8,9},{9,8},{10,11... | collective-permute-start | bytes 1966088 | tf_op jit(solution)/shard_map/ppermute | solution.py:16
  61.0 3.4 %shard_map.58 = bf16[4,2,32,1408]{3,2,1,0:T(8,128)(2,1)S(1)} custom-call(s32[2]{0:T(128)S(1)} %pad_add_fusion.place, bf16[2,256,640]{2,1,0:T(8,128)(2,1)} %bitcast.4.g_own.g_other, bf16[2,256,640]{2,1,0:T(8,128)(2,1)} %bitcast.4.g_own.g_other, bf16[2,256,640]{2,1,0:T(8,128)(2,1)} %collective-permute-done.2.s_own.s_other, ...), custom_call_target="tpu_custom_call" | custom-call | flops 850000000 | bytes 5000000 | tf_op jit(solution)/shard_map/pallas_call | solution.py:51
  65.3 11.3 %all-to-all-start.1 = ((bf16[16,16,1408]{2,1,0:T(8,128)(2,1)}), bf16[16,16,1408]{2,1,0:T(8,128)(2,1)}, u32[]{:S(2)}, u32[]{:S(2)}) async-start(bf16[16,16,1408]{2,1,0:T(8,128)(2,1)} %bitcast.55), calls=%async_computation.1 | async-start | bytes 1441792 | tf_op jit(solution)/shard_map/all_to_all | solution.py:109
  76.6 1.0 constant_dynamic-slice_fusion.2
  78.5 1.2 %maximum_add_fusion = f32[2,128,640]{2,1,0:T(8,128)S(1)} fusion(f32[2,128,640]{2,1,0:T(8,128)} %collective-permute-done.3, f32[1,128,640]{2,1,0:T(8,128)S(1)} %convolution_bitcast_fusion, f32[1,128,640]{2,1,0:T(8,128)S(1)} %convolution_bitcast_fusion.1), kind=kLoop, calls=%fused_computation.8 | loop fusion | flops 327680 | bytes 1966080 | tf_op jit(solution)/shard_map/add | solution.py:112
  79.8 4.4 %collective-permute-start.4 = (f32[2,32,640]{2,1,0:T(8,128)S(1)}, f32[2,32,640]{2,1,0:T(8,128)S(1)}, u32[]{:S(2)}, u32[]{:S(2)}) collective-permute-start(f32[2,32,640]{2,1,0:T(8,128)S(1)} %get-tuple-element.23), channel_id=1, source_target_pairs={{0,2},{2,0},{1,3},{3,1},{4,6},{6,4},{5,7},{7,5},{8,10},{10,8},{9,1... | collective-permute-start | bytes 491528 | tf_op jit(solution)/shard_map/ppermute | solution.py:16
  84.2 2.4 %collective-permute-start.5 = (f32[2,32,640]{2,1,0:T(8,128)S(1)}, f32[2,32,640]{2,1,0:T(8,128)S(1)}, u32[]{:S(2)}, u32[]{:S(2)}) collective-permute-start(f32[2,32,640]{2,1,0:T(8,128)S(1)} %get-tuple-element.25), channel_id=1, source_target_pairs={{0,4},{4,0},{1,5},{5,1},{2,6},{6,2},{3,7},{7,3},{8,12},{12,8},{9,1... | collective-permute-start | bytes 491528 | tf_op jit(solution)/shard_map/ppermute | solution.py:16
  86.6 4.0 %collective-permute-start.6 = (f32[2,32,640]{2,1,0:T(8,128)S(1)}, f32[2,32,640]{2,1,0:T(8,128)S(1)}, u32[]{:S(2)}, u32[]{:S(2)}) collective-permute-start(f32[2,32,640]{2,1,0:T(8,128)S(1)} %get-tuple-element.24), channel_id=1, source_target_pairs={{0,6},{2,4},{4,2},{6,0},{1,7},{3,5},{5,3},{7,1},{8,14},{10,12},{12... | collective-permute-start | bytes 491528 | tf_op jit(solution)/shard_map/ppermute | solution.py:115
  90.6 1.5 %maximum_select_fusion = bf16[2,256,1280]{2,1,0:T(8,128)(2,1)S(1)} fusion(bf16[1,256,1280]{2,1,0:T(8,128)(2,1)} %bitcast.20, bf16[1,256,1280]{2,1,0:T(8,128)(2,1)S(1)} %bitcast.58, pred[]{:T(512)S(6)} %eq.10), kind=kLoop, calls=%fused_computation.2 | loop fusion | flops 1966080 | bytes 2621441 | tf_op jit(solution)/shard_map/jit(_where)/select_n | solution.py:24
  92.1 1.1 constant_dynamic-slice_fusion
  93.4 3.1 %collective-permute-done.6 = f32[2,32,640]{2,1,0:T(8,128)S(1)} collective-permute-done((f32[2,32,640]{2,1,0:T(8,128)S(1)}, f32[2,32,640]{2,1,0:T(8,128)S(1)}, u32[]{:S(2)}, u32[]{:S(2)}) %collective-permute-start.6) | collective-permute-done | bytes 163872 | tf_op jit(solution)/shard_map/ppermute | solution.py:115
  96.5 4.0 %collective-permute-start.7 = (f32[32,640]{1,0:T(8,128)S(1)}, f32[32,640]{1,0:T(8,128)S(1)}, u32[]{:S(2)}, u32[]{:S(2)}) collective-permute-start(f32[32,640]{1,0:T(8,128)S(1)} %fusion.3), channel_id=1, source_target_pairs={{0,256},{8,0},{256,264},{264,8},{1,257},{9,1},{257,265},{265,9},{2... | collective-permute-start | bytes 245768 | tf_op jit(solution)/shard_map/ppermute | solution.py:118
  100.5 2.5 %collective-permute-start.8 = (f32[32,640]{1,0:T(8,128)S(1)}, f32[32,640]{1,0:T(8,128)S(1)}, u32[]{:S(2)}, u32[]{:S(2)}) collective-permute-start(f32[32,640]{1,0:T(8,128)S(1)} %slice_bitcast_fusion.1), channel_id=1, source_target_pairs={{8,256},{256,8},{9,257},{257,9},{10,258},{258,10},{11,259},{259,11... | collective-permute-start | bytes 245768 | tf_op jit(solution)/shard_map/ppermute | solution.py:119
  103.0 2.4 %fusion = bf16[1280,640]{1,0:T(8,128)(2,1)} fusion(bf16[512,1280]{1,0:T(8,128)(2,1)S(1)} %bitcast.65, bf16[512,640]{1,0:T(8,128)(2,1)S(1)} %bitcast.68), kind=kOutput, calls=%fused_computation.1 | convolution fusion | flops 840499200 | bytes 3604480 | tf_op jit(solution)/shard_map/dot_general | solution.py:126
  105.4 3.9 %collective-permute-done.8 = f32[32,640]{1,0:T(8,128)S(1)} collective-permute-done((f32[32,640]{1,0:T(8,128)S(1)}, f32[32,640]{1,0:T(8,128)S(1)}, u32[]{:S(2)}, u32[]{:S(2)}) %collective-permute-start.8) | collective-permute-done | bytes 81952 | tf_op jit(solution)/shard_map/ppermute | solution.py:119
  109.8 4.5 %all-to-all-done.1.parts.powers = bf16[16,16,1408]{2,1,0:T(8,128)(2,1)} async-done(((bf16[16,16,1408]{2,1,0:T(8,128)(2,1)}), bf16[16,16,1408]{2,1,0:T(8,128)(2,1)}, u32[]{:S(2)}, u32[]{:S(2)}) %all-to-all-start.1) | async-done | bytes 720928 | tf_op jit(solution)/shard_map/all_to_all | solution.py:109
  114.3 2.3 %shard_map.59 = bf16[16,1280]{1,0:T(8,128)(2,1)} custom-call(bf16[16,16,1408]{2,1,0:T(8,128)(2,1)} %all-to-all-done.1.parts.powers, bf16[16,16,1408]{2,1,0:T(8,128)(2,1)} %all-to-all-done.1.parts.powers), custom_call_target="tpu_custom_call" | custom-call | tf_op jit(solution)/shard_map/pallas_call | solution.py:77
  (30 shorter events, 3.6 us)
Async XLA Ops:
  0.6 52.0 %copy-start = (bf16[1280,640]{1,0:T(8,128)(2,1)S(1)}, bf16[1280,640]{1,0:T(8,128)(2,1)}, u32[]{:S(2)}) copy-start(bf16[1280,640]{1,0:T(8,128)(2,1)} %w_own.1) | copy-start | bytes 4915204
  0.6 13.7 %copy-start.4 = (bf16[16,1280]{1,0:T(8,128)(2,1)S(1)}, bf16[16,1280]{1,0:T(8,128)(2,1)}, u32[]{:S(2)}) copy-start(bf16[16,1280]{1,0:T(8,128)(2,1)} %param.3) | copy-start | bytes 122884
  0.7 51.9 %collective-permute-start = (bf16[1280,640]{1,0:T(8,128)(2,1)}, bf16[1280,640]{1,0:T(8,128)(2,1)S(1)}, u32[]{:S(2)}, u32[]{:S(2)}) collective-permute-start(bf16[1280,640]{1,0:T(8,128)(2,1)} %w_own.1), channel_id=1, source_target_pairs={{0,256},{256,0},{1,257},{257,1},{2,258},{258,2},{3,259},{259,3},{4... | collective-permute-start | bytes 4915208 | tf_op jit(solution)/shard_map/ppermute | solution.py:16
  5.2 49.2 %all-to-all-start = ((bf16[16,32,640]{2,1,0:T(8,128)(2,1)}), bf16[16,32,640]{2,1,0:T(8,128)(2,1)}, u32[]{:S(2)}, u32[]{:S(2)}) async-start(bf16[16,32,640]{2,1,0:T(8,128)(2,1)} %broadcast_in_dim.2), calls=%async_computation | async-start | bytes 1310720 | tf_op jit(solution)/shard_map/all_to_all | solution.py:95
  52.5 0.9 copy-start.2
  54.4 6.6 %collective-permute-start.2 = (bf16[2,256,640]{2,1,0:T(8,128)(2,1)}, bf16[2,256,640]{2,1,0:T(8,128)(2,1)}, u32[]{:S(2)}, u32[]{:S(2)}) collective-permute-start(bf16[2,256,640]{2,1,0:T(8,128)(2,1)} %bitcast.4.g_own.g_other), channel_id=1, source_target_pairs={{0,1},{1,0},{2,3},{3,2},{4,5},{5,4},{6,7},{7,6},{8,9},{9,8},{10,11... | collective-permute-start | bytes 1966088 | tf_op jit(solution)/shard_map/ppermute | solution.py:16
  56.4 23.4 %collective-permute-start.1 = (bf16[256,1280]{1,0:T(8,128)(2,1)}, bf16[256,1280]{1,0:T(8,128)(2,1)}, u32[]{:S(2)}, u32[]{:S(2)}) collective-permute-start(bf16[256,1280]{1,0:T(8,128)(2,1)} %copy-done.2), channel_id=1, source_target_pairs={{0,256},{256,0},{1,257},{257,1},{2,258},{258,2},{3,259},{259,3},{4... | collective-permute-start | bytes 1966088 | tf_op jit(solution)/shard_map/ppermute | solution.py:16
  58.9 19.7 %collective-permute-start.3 = (f32[2,128,640]{2,1,0:T(8,128)}, f32[2,128,640]{2,1,0:T(8,128)}, u32[]{:S(2)}, u32[]{:S(2)}) collective-permute-start(f32[2,128,640]{2,1,0:T(8,128)} %pad_maximum_fusion), channel_id=1, source_target_pairs={{0,1},{1,0},{2,3},{3,2},{4,5},{5,4},{6,7},{7,6},{8,9},{9,8},{10,11... | collective-permute-start | bytes 1966088 | tf_op jit(solution)/shard_map/ppermute | solution.py:16
  64.4 0.9 copy-start.1
  65.3 49.0 %all-to-all-start.1 = ((bf16[16,16,1408]{2,1,0:T(8,128)(2,1)}), bf16[16,16,1408]{2,1,0:T(8,128)(2,1)}, u32[]{:S(2)}, u32[]{:S(2)}) async-start(bf16[16,16,1408]{2,1,0:T(8,128)(2,1)} %bitcast.55), calls=%async_computation.1 | async-start | bytes 1441792 | tf_op jit(solution)/shard_map/all_to_all | solution.py:109
  78.5 12.0 %copy-start.3 = (bf16[256,1280]{1,0:T(8,128)(2,1)S(1)}, bf16[256,1280]{1,0:T(8,128)(2,1)}, u32[]{:S(2)}) copy-start(bf16[256,1280]{1,0:T(8,128)(2,1)} %copy-done.2) | copy-start | bytes 1966084
  79.8 13.5 %collective-permute-start.4 = (f32[2,32,640]{2,1,0:T(8,128)S(1)}, f32[2,32,640]{2,1,0:T(8,128)S(1)}, u32[]{:S(2)}, u32[]{:S(2)}) collective-permute-start(f32[2,32,640]{2,1,0:T(8,128)S(1)} %get-tuple-element.23), channel_id=1, source_target_pairs={{0,2},{2,0},{1,3},{3,1},{4,6},{6,4},{5,7},{7,5},{8,10},{10,8},{9,1... | collective-permute-start | bytes 491528 | tf_op jit(solution)/shard_map/ppermute | solution.py:16
  84.2 9.2 %collective-permute-start.5 = (f32[2,32,640]{2,1,0:T(8,128)S(1)}, f32[2,32,640]{2,1,0:T(8,128)S(1)}, u32[]{:S(2)}, u32[]{:S(2)}) collective-permute-start(f32[2,32,640]{2,1,0:T(8,128)S(1)} %get-tuple-element.25), channel_id=1, source_target_pairs={{0,4},{4,0},{1,5},{5,1},{2,6},{6,2},{3,7},{7,3},{8,12},{12,8},{9,1... | collective-permute-start | bytes 491528 | tf_op jit(solution)/shard_map/ppermute | solution.py:16
  86.6 9.9 %collective-permute-start.6 = (f32[2,32,640]{2,1,0:T(8,128)S(1)}, f32[2,32,640]{2,1,0:T(8,128)S(1)}, u32[]{:S(2)}, u32[]{:S(2)}) collective-permute-start(f32[2,32,640]{2,1,0:T(8,128)S(1)} %get-tuple-element.24), channel_id=1, source_target_pairs={{0,6},{2,4},{4,2},{6,0},{1,7},{3,5},{5,3},{7,1},{8,14},{10,12},{12... | collective-permute-start | bytes 491528 | tf_op jit(solution)/shard_map/ppermute | solution.py:115
  96.5 8.9 %collective-permute-start.7 = (f32[32,640]{1,0:T(8,128)S(1)}, f32[32,640]{1,0:T(8,128)S(1)}, u32[]{:S(2)}, u32[]{:S(2)}) collective-permute-start(f32[32,640]{1,0:T(8,128)S(1)} %fusion.3), channel_id=1, source_target_pairs={{0,256},{8,0},{256,264},{264,8},{1,257},{9,1},{257,265},{265,9},{2... | collective-permute-start | bytes 245768 | tf_op jit(solution)/shard_map/ppermute | solution.py:118
  100.5 8.7 %collective-permute-start.8 = (f32[32,640]{1,0:T(8,128)S(1)}, f32[32,640]{1,0:T(8,128)S(1)}, u32[]{:S(2)}, u32[]{:S(2)}) collective-permute-start(f32[32,640]{1,0:T(8,128)S(1)} %slice_bitcast_fusion.1), channel_id=1, source_target_pairs={{8,256},{256,8},{9,257},{257,9},{10,258},{258,10},{11,259},{259,11... | collective-permute-start | bytes 245768 | tf_op jit(solution)/shard_map/ppermute | solution.py:119

commit v6 on v5

--- a/solution.py
+++ b/solution.py
@@ -105,7 +105,7 @@
     swapped = swap(grads, "core")
     coded = encode(grads, swapped, xl, core, weight, weight_other)
     own_other = swap(own, "xl")
-    own, grads, swapped, coded = lax.optimization_barrier((own, grads, swapped, coded))
+    own, grads, swapped, sent, coded = lax.optimization_barrier((own, grads, swapped, sent, coded))
     parts = lax.all_to_all(coded.reshape(16, 16, 1408), "z", 0, 0, tiled=True)
     input_grad = decode(parts)
 

time: 118 us -> 118 us (level)
    ppermute x1, waiting for transfers between devices: 3.05 us -> 4.32 us  [on_device(): lax.ppermute(piece(1 - yl, 1 - xh), ('yl', 'xh'), [(0, 3), (1, 2), (2, 1)...]
  transfers between devices with their start and end apart: 11 -> 11, of which waited for: 3 -> 3; matrix products, arithmetic and copies ran while one was open for 11% -> 10% of each run, Pallas kernels for 3% -> 3%
where the time goes in v6:
time: 118 us; the launch traced here: 117 us
  starting transfers between devices  47 us (40%)
  blocking collectives  38.3 us (32%)
  waiting for transfers between devices  12.3 us (10%)
  Pallas kernels  5.69 us (5%)
  other arithmetic  4.39 us (4%)
  matrix products  4.11 us (3%)
  local copies, waits for them, and re-layouts  3.88 us (3%)
    all_gather x1, blocking collectives, on_device(): own = lax.all_gather(inputs, 'z', axis=0, tiled=True)  38.3 us
    ppermute x6, starting transfers between devices, swap(): return lax.ppermute(x, axis, [(0, 1), (1, 0)])  16.1 us
    all_to_all x1, starting transfers between devices, on_device(): parts = lax.all_to_all(coded.reshape(16, 16, 1408), 'z', 0, 0, tiled=True)  11.3 us
    all_to_all x1, starting transfers between devices, on_device(): lax.all_to_all(spread, ('xl',) + COL[:3], 0, 0, tiled=True)  9.09 us
    ppermute x1, waiting for transfers between devices, on_device(): lax.ppermute(piece(1 - yl, 1 - xh), ('yl', 'xh'), [(0, 3), (1, 2), (2, 1)...  4.32 us
    all_to_all x1, waiting for transfers between devices, on_device(): parts = lax.all_to_all(coded.reshape(16, 16, 1408), 'z', 0, 0, tiled=True)  4.19 us
    ppermute x1, starting transfers between devices, on_device(): lax.ppermute(piece(1 - yl, 1 - xh), ('yl', 'xh'), [(0, 3), (1, 2), (2, 1)...  3.99 us
    ppermute x1, starting transfers between devices, on_device(): lax.ppermute(jnp.where(same, q[1], q[0]), ('xl', 'yh'), [(0, 2), (1, 0),...  3.97 us
  transfers between devices with their start and end apart: 11, of which 3 were waited for; matrix products, arithmetic and copies ran while one was open for 10% of the time, Pallas kernels for 3%

profile of v6, /device:TPU:6, one launch (start us, length us, event | category | flops | bytes accessed | tf_op | source)
XLA Modules:
  0.0 116.6 jit_solution(7909334072555201988)
XLA Ops:
  0.7 2.9 %collective-permute-start = (bf16[1280,640]{1,0:T(8,128)(2,1)}, bf16[1280,640]{1,0:T(8,128)(2,1)S(1)}, u32[]{:S(2)}, u32[]{:S(2)}) collective-permute-start(bf16[1280,640]{1,0:T(8,128)(2,1)} %w_own.1), channel_id=1, source_target_pairs={{0,256},{256,0},{1,257},{257,1},{2,258},{258,2},{3,259},{259,3},{4... | collective-permute-start | bytes 4915208 | tf_op jit(solution)/shard_map/ppermute | solution.py:16
  3.5 1.7 %broadcast_in_dim.2 = bf16[16,32,640]{2,1,0:T(8,128)(2,1)} broadcast(bf16[32,640]{1,0:T(8,128)(2,1)} %param.5), dimensions={1,2} | broadcast | bytes 696320 | tf_op jit(solution)/shard_map/broadcast_in_dim | solution.py:94
  5.2 9.1 %all-to-all-start = ((bf16[16,32,640]{2,1,0:T(8,128)(2,1)}), bf16[16,32,640]{2,1,0:T(8,128)(2,1)}, u32[]{:S(2)}, u32[]{:S(2)}) async-start(bf16[16,32,640]{2,1,0:T(8,128)(2,1)} %broadcast_in_dim.2), calls=%async_computation | async-start | bytes 1310720 | tf_op jit(solution)/shard_map/all_to_all | solution.py:95
  14.3 38.3 %all_gather.3 = bf16[256,1280]{1,0:T(8,128)(2,1)S(1)} all-gather(bf16[16,1280]{1,0:T(8,128)(2,1)S(1)} %copy-done.4), channel_id=1, replica_groups=mesh['xl'=2,'z'=16,'yh'=2,'yl'=2,'xh'=2,'core'=2] {'z'}, dimensions={0}, use_global_device_ids=true | all-gather | bytes 696320 | tf_op jit(solution)/shard_map/all_gather | solution.py:97
  53.5 0.9 pad_maximum_fusion
  54.4 1.9 %collective-permute-start.2 = (bf16[2,256,640]{2,1,0:T(8,128)(2,1)}, bf16[2,256,640]{2,1,0:T(8,128)(2,1)}, u32[]{:S(2)}, u32[]{:S(2)}) collective-permute-start(bf16[2,256,640]{2,1,0:T(8,128)(2,1)} %bitcast.4.g_own.g_other), channel_id=1, source_target_pairs={{0,1},{1,0},{2,3},{3,2},{4,5},{5,4},{6,7},{7,6},{8,9},{9,8},{10,11... | collective-permute-start | bytes 1966088 | tf_op jit(solution)/shard_map/ppermute | solution.py:16
  56.4 2.5 %collective-permute-start.1 = (bf16[256,1280]{1,0:T(8,128)(2,1)}, bf16[256,1280]{1,0:T(8,128)(2,1)}, u32[]{:S(2)}, u32[]{:S(2)}) collective-permute-start(bf16[256,1280]{1,0:T(8,128)(2,1)} %copy-done.2), channel_id=1, source_target_pairs={{0,256},{256,0},{1,257},{257,1},{2,258},{258,2},{3,259},{259,3},{4... | collective-permute-start | bytes 1966088 | tf_op jit(solution)/shard_map/ppermute | solution.py:16
  58.9 3.4 %shard_map.58 = bf16[4,2,32,1408]{3,2,1,0:T(8,128)(2,1)S(1)} custom-call(s32[2]{0:T(128)S(1)} %pad_add_fusion.place, bf16[2,256,640]{2,1,0:T(8,128)(2,1)} %bitcast.4.g_own.g_other, bf16[2,256,640]{2,1,0:T(8,128)(2,1)} %bitcast.4.g_own.g_other, bf16[2,256,640]{2,1,0:T(8,128)(2,1)} %collective-permute-done.2.s_own.s_other, ...), custom_call_target="tpu_custom_call" | custom-call | flops 850000000 | bytes 5000000 | tf_op jit(solution)/shard_map/pallas_call | solution.py:51
  62.3 0.9 copy-done.1
  63.2 2.1 %collective-permute-start.3 = (f32[2,128,640]{2,1,0:T(8,128)}, f32[2,128,640]{2,1,0:T(8,128)}, u32[]{:S(2)}, u32[]{:S(2)}) collective-permute-start(f32[2,128,640]{2,1,0:T(8,128)} %pad_maximum_fusion), channel_id=1, source_target_pairs={{0,1},{1,0},{2,3},{3,2},{4,5},{5,4},{6,7},{7,6},{8,9},{9,8},{10,11... | collective-permute-start | bytes 1966088 | tf_op jit(solution)/shard_map/ppermute | solution.py:16
  65.3 11.3 %all-to-all-start.1 = ((bf16[16,16,1408]{2,1,0:T(8,128)(2,1)}), bf16[16,16,1408]{2,1,0:T(8,128)(2,1)}, u32[]{:S(2)}, u32[]{:S(2)}) async-start(bf16[16,16,1408]{2,1,0:T(8,128)(2,1)} %bitcast.55), calls=%async_computation.1 | async-start | bytes 1441792 | tf_op jit(solution)/shard_map/all_to_all | solution.py:109
  76.6 1.2 %constant_dynamic-slice_fusion = (bf16[1,256,640]{2,1,0:T(8,128)(2,1)S(1)}, bf16[1,256,640]{2,1,0:T(8,128)(2,1)S(1)}) fusion(bf16[2,256,640]{2,1,0:T(8,128)(2,1)} %collective-permute-done.2.s_own.s_other, s32[]{:T(128)S(6)} %select_n.103, bf16[2,256,640]{2,1,0:T(8,128)(2,1)} %bitcast.4.g_own.g_other), kind=kLoop, calls=%fused_computation.20 | loop fusion | bytes 1310724 | tf_op jit(solution)/shard_map/jit(dynamic_index_in_dim)/dynamic_slice | solution.py:20
  78.9 1.2 maximum_add_fusion
  80.1 4.4 %collective-permute-start.4 = (f32[2,32,640]{2,1,0:T(8,128)S(1)}, f32[2,32,640]{2,1,0:T(8,128)S(1)}, u32[]{:S(2)}, u32[]{:S(2)}) collective-permute-start(f32[2,32,640]{2,1,0:T(8,128)S(1)} %get-tuple-element.25), channel_id=1, source_target_pairs={{0,2},{2,0},{1,3},{3,1},{4,6},{6,4},{5,7},{7,5},{8,10},{10,8},{9,1... | collective-permute-start | bytes 491528 | tf_op jit(solution)/shard_map/ppermute | solution.py:16
  84.5 2.4 %collective-permute-start.5 = (f32[2,32,640]{2,1,0:T(8,128)S(1)}, f32[2,32,640]{2,1,0:T(8,128)S(1)}, u32[]{:S(2)}, u32[]{:S(2)}) collective-permute-start(f32[2,32,640]{2,1,0:T(8,128)S(1)} %get-tuple-element.27), channel_id=1, source_target_pairs={{0,4},{4,0},{1,5},{5,1},{2,6},{6,2},{3,7},{7,3},{8,12},{12,8},{9,1... | collective-permute-start | bytes 491528 | tf_op jit(solution)/shard_map/ppermute | solution.py:16
  86.8 4.0 %collective-permute-start.6 = (f32[2,32,640]{2,1,0:T(8,128)S(1)}, f32[2,32,640]{2,1,0:T(8,128)S(1)}, u32[]{:S(2)}, u32[]{:S(2)}) collective-permute-start(f32[2,32,640]{2,1,0:T(8,128)S(1)} %get-tuple-element.26), channel_id=1, source_target_pairs={{0,6},{2,4},{4,2},{6,0},{1,7},{3,5},{5,3},{7,1},{8,14},{10,12},{12... | collective-permute-start | bytes 491528 | tf_op jit(solution)/shard_map/ppermute | solution.py:115
  90.8 1.5 %maximum_select_fusion = bf16[2,256,1280]{2,1,0:T(8,128)(2,1)S(1)} fusion(bf16[1,256,1280]{2,1,0:T(8,128)(2,1)} %bitcast.20, bf16[1,256,1280]{2,1,0:T(8,128)(2,1)S(1)} %bitcast.58, pred[]{:T(512)S(6)} %eq.10), kind=kLoop, calls=%fused_computation.2 | loop fusion | flops 1966080 | bytes 2621441 | tf_op jit(solution)/shard_map/jit(_where)/select_n | solution.py:24
  92.4 4.3 %collective-permute-done.6 = f32[2,32,640]{2,1,0:T(8,128)S(1)} collective-permute-done((f32[2,32,640]{2,1,0:T(8,128)S(1)}, f32[2,32,640]{2,1,0:T(8,128)S(1)}, u32[]{:S(2)}, u32[]{:S(2)}) %collective-permute-start.6) | collective-permute-done | bytes 163872 | tf_op jit(solution)/shard_map/ppermute | solution.py:115
  96.8 4.0 %collective-permute-start.7 = (f32[32,640]{1,0:T(8,128)S(1)}, f32[32,640]{1,0:T(8,128)S(1)}, u32[]{:S(2)}, u32[]{:S(2)}) collective-permute-start(f32[32,640]{1,0:T(8,128)S(1)} %fusion.3), channel_id=1, source_target_pairs={{0,256},{8,0},{256,264},{264,8},{1,257},{9,1},{257,265},{265,9},{2... | collective-permute-start | bytes 245768 | tf_op jit(solution)/shard_map/ppermute | solution.py:118
  100.7 2.6 %collective-permute-start.8 = (f32[32,640]{1,0:T(8,128)S(1)}, f32[32,640]{1,0:T(8,128)S(1)}, u32[]{:S(2)}, u32[]{:S(2)}) collective-permute-start(f32[32,640]{1,0:T(8,128)S(1)} %slice_bitcast_fusion.1), channel_id=1, source_target_pairs={{8,256},{256,8},{9,257},{257,9},{10,258},{258,10},{11,259},{259,11... | collective-permute-start | bytes 245768 | tf_op jit(solution)/shard_map/ppermute | solution.py:119
  103.3 2.4 %fusion = bf16[1280,640]{1,0:T(8,128)(2,1)} fusion(bf16[512,1280]{1,0:T(8,128)(2,1)S(1)} %bitcast.65, bf16[512,640]{1,0:T(8,128)(2,1)S(1)} %bitcast.68), kind=kOutput, calls=%fused_computation.1 | convolution fusion | flops 840499200 | bytes 3604480 | tf_op jit(solution)/shard_map/dot_general | solution.py:126
  105.7 3.8 %collective-permute-done.8 = f32[32,640]{1,0:T(8,128)S(1)} collective-permute-done((f32[32,640]{1,0:T(8,128)S(1)}, f32[32,640]{1,0:T(8,128)S(1)}, u32[]{:S(2)}, u32[]{:S(2)}) %collective-permute-start.8) | collective-permute-done | bytes 81952 | tf_op jit(solution)/shard_map/ppermute | solution.py:119
  110.1 4.2 %all-to-all-done.1.parts.powers = bf16[16,16,1408]{2,1,0:T(8,128)(2,1)} async-done(((bf16[16,16,1408]{2,1,0:T(8,128)(2,1)}), bf16[16,16,1408]{2,1,0:T(8,128)(2,1)}, u32[]{:S(2)}, u32[]{:S(2)}) %all-to-all-start.1) | async-done | bytes 720928 | tf_op jit(solution)/shard_map/all_to_all | solution.py:109
  114.3 2.3 %shard_map.59 = bf16[16,1280]{1,0:T(8,128)(2,1)} custom-call(bf16[16,16,1408]{2,1,0:T(8,128)(2,1)} %all-to-all-done.1.parts.powers, bf16[16,16,1408]{2,1,0:T(8,128)(2,1)} %all-to-all-done.1.parts.powers), custom_call_target="tpu_custom_call" | custom-call | tf_op jit(solution)/shard_map/pallas_call | solution.py:77
  (30 shorter events, 2.7 us)
Async XLA Ops:
  0.6 52.0 %copy-start = (bf16[1280,640]{1,0:T(8,128)(2,1)S(1)}, bf16[1280,640]{1,0:T(8,128)(2,1)}, u32[]{:S(2)}) copy-start(bf16[1280,640]{1,0:T(8,128)(2,1)} %w_own.1) | copy-start | bytes 4915204
  0.6 13.7 %copy-start.4 = (bf16[16,1280]{1,0:T(8,128)(2,1)S(1)}, bf16[16,1280]{1,0:T(8,128)(2,1)}, u32[]{:S(2)}) copy-start(bf16[16,1280]{1,0:T(8,128)(2,1)} %param.3) | copy-start | bytes 122884
  0.7 51.9 %collective-permute-start = (bf16[1280,640]{1,0:T(8,128)(2,1)}, bf16[1280,640]{1,0:T(8,128)(2,1)S(1)}, u32[]{:S(2)}, u32[]{:S(2)}) collective-permute-start(bf16[1280,640]{1,0:T(8,128)(2,1)} %w_own.1), channel_id=1, source_target_pairs={{0,256},{256,0},{1,257},{257,1},{2,258},{258,2},{3,259},{259,3},{4... | collective-permute-start | bytes 4915208 | tf_op jit(solution)/shard_map/ppermute | solution.py:16
  5.2 49.2 %all-to-all-start = ((bf16[16,32,640]{2,1,0:T(8,128)(2,1)}), bf16[16,32,640]{2,1,0:T(8,128)(2,1)}, u32[]{:S(2)}, u32[]{:S(2)}) async-start(bf16[16,32,640]{2,1,0:T(8,128)(2,1)} %broadcast_in_dim.2), calls=%async_computation | async-start | bytes 1310720 | tf_op jit(solution)/shard_map/all_to_all | solution.py:95
  52.6 0.9 copy-start.2
  54.4 4.5 %collective-permute-start.2 = (bf16[2,256,640]{2,1,0:T(8,128)(2,1)}, bf16[2,256,640]{2,1,0:T(8,128)(2,1)}, u32[]{:S(2)}, u32[]{:S(2)}) collective-permute-start(bf16[2,256,640]{2,1,0:T(8,128)(2,1)} %bitcast.4.g_own.g_other), channel_id=1, source_target_pairs={{0,1},{1,0},{2,3},{3,2},{4,5},{5,4},{6,7},{7,6},{8,9},{9,8},{10,11... | collective-permute-start | bytes 1966088 | tf_op jit(solution)/shard_map/ppermute | solution.py:16
  56.4 23.6 %collective-permute-start.1 = (bf16[256,1280]{1,0:T(8,128)(2,1)}, bf16[256,1280]{1,0:T(8,128)(2,1)}, u32[]{:S(2)}, u32[]{:S(2)}) collective-permute-start(bf16[256,1280]{1,0:T(8,128)(2,1)} %copy-done.2), channel_id=1, source_target_pairs={{0,256},{256,0},{1,257},{257,1},{2,258},{258,2},{3,259},{259,3},{4... | collective-permute-start | bytes 1966088 | tf_op jit(solution)/shard_map/ppermute | solution.py:16
  62.3 0.9 copy-start.1
  63.2 15.7 %collective-permute-start.3 = (f32[2,128,640]{2,1,0:T(8,128)}, f32[2,128,640]{2,1,0:T(8,128)}, u32[]{:S(2)}, u32[]{:S(2)}) collective-permute-start(f32[2,128,640]{2,1,0:T(8,128)} %pad_maximum_fusion), channel_id=1, source_target_pairs={{0,1},{1,0},{2,3},{3,2},{4,5},{5,4},{6,7},{7,6},{8,9},{9,8},{10,11... | collective-permute-start | bytes 1966088 | tf_op jit(solution)/shard_map/ppermute | solution.py:16
  65.3 49.0 %all-to-all-start.1 = ((bf16[16,16,1408]{2,1,0:T(8,128)(2,1)}), bf16[16,16,1408]{2,1,0:T(8,128)(2,1)}, u32[]{:S(2)}, u32[]{:S(2)}) async-start(bf16[16,16,1408]{2,1,0:T(8,128)(2,1)} %bitcast.55), calls=%async_computation.1 | async-start | bytes 1441792 | tf_op jit(solution)/shard_map/all_to_all | solution.py:109
  76.6 1.3 %copy-start.3 = (bf16[256,1280]{1,0:T(8,128)(2,1)S(1)}, bf16[256,1280]{1,0:T(8,128)(2,1)}, u32[]{:S(2)}) copy-start(bf16[256,1280]{1,0:T(8,128)(2,1)} %copy-done.2) | copy-start | bytes 1966084
  80.1 12.3 %collective-permute-start.4 = (f32[2,32,640]{2,1,0:T(8,128)S(1)}, f32[2,32,640]{2,1,0:T(8,128)S(1)}, u32[]{:S(2)}, u32[]{:S(2)}) collective-permute-start(f32[2,32,640]{2,1,0:T(8,128)S(1)} %get-tuple-element.25), channel_id=1, source_target_pairs={{0,2},{2,0},{1,3},{3,1},{4,6},{6,4},{5,7},{7,5},{8,10},{10,8},{9,1... | collective-permute-start | bytes 491528 | tf_op jit(solution)/shard_map/ppermute | solution.py:16
  84.5 7.9 %collective-permute-start.5 = (f32[2,32,640]{2,1,0:T(8,128)S(1)}, f32[2,32,640]{2,1,0:T(8,128)S(1)}, u32[]{:S(2)}, u32[]{:S(2)}) collective-permute-start(f32[2,32,640]{2,1,0:T(8,128)S(1)} %get-tuple-element.27), channel_id=1, source_target_pairs={{0,4},{4,0},{1,5},{5,1},{2,6},{6,2},{3,7},{7,3},{8,12},{12,8},{9,1... | collective-permute-start | bytes 491528 | tf_op jit(solution)/shard_map/ppermute | solution.py:16
  86.8 9.9 %collective-permute-start.6 = (f32[2,32,640]{2,1,0:T(8,128)S(1)}, f32[2,32,640]{2,1,0:T(8,128)S(1)}, u32[]{:S(2)}, u32[]{:S(2)}) collective-permute-start(f32[2,32,640]{2,1,0:T(8,128)S(1)} %get-tuple-element.26), channel_id=1, source_target_pairs={{0,6},{2,4},{4,2},{6,0},{1,7},{3,5},{5,3},{7,1},{8,14},{10,12},{12... | collective-permute-start | bytes 491528 | tf_op jit(solution)/shard_map/ppermute | solution.py:115
  96.8 9.0 %collective-permute-start.7 = (f32[32,640]{1,0:T(8,128)S(1)}, f32[32,640]{1,0:T(8,128)S(1)}, u32[]{:S(2)}, u32[]{:S(2)}) collective-permute-start(f32[32,640]{1,0:T(8,128)S(1)} %fusion.3), channel_id=1, source_target_pairs={{0,256},{8,0},{256,264},{264,8},{1,257},{9,1},{257,265},{265,9},{2... | collective-permute-start | bytes 245768 | tf_op jit(solution)/shard_map/ppermute | solution.py:118
  100.7 8.7 %collective-permute-start.8 = (f32[32,640]{1,0:T(8,128)S(1)}, f32[32,640]{1,0:T(8,128)S(1)}, u32[]{:S(2)}, u32[]{:S(2)}) collective-permute-start(f32[32,640]{1,0:T(8,128)S(1)} %slice_bitcast_fusion.1), channel_id=1, source_target_pairs={{8,256},{256,8},{9,257},{257,9},{10,258},{258,10},{11,259},{259,11... | collective-permute-start | bytes 245768 | tf_op jit(solution)/shard_map/ppermute | solution.py:119
